TPU v7x, 32 devices: a whole 2x2x4 slice. The times are simulated.
32 devices in a mesh: section: 2 (over core), dp: 16 (over z, y, x).
Axes of the slice: x: 2, y: 2, z: 4, core: 2. Of those that a mesh axis runs over, the one named last changes fastest.
Arguments:
- node_input: bfloat16 [2, 2048, 128], P(None, 'dp'), may hold values from -6 to 6
- edge_input: bfloat16 [2, 16, 10240], P(None, None, 'dp'), may hold values from -6 to 6
- edge_source: int32 [2, 10240], P(None, 'dp'), may hold values from 0 to 127, as said below
- edge_target: int32 [2, 10240], P(None, 'dp'), may hold values from 0 to 127, as said below
- edge_valid: int32 [2, 10240], P(None, 'dp'), may hold values 0 or 1
- node_labeled: int32 [2, 2048], P(None, 'dp'), may hold values from 0 to 1, as said below
- edge_w1: bfloat16 [16, 128], replicated, may hold values from -1.5 to 1.5
- edge_b1: bfloat16 [128], replicated, may hold values from -3 to 3
- edge_w2: bfloat16 [128, 16384], replicated, may hold values from -0.046875 to 0.046875
- edge_b2: bfloat16 [16384], replicated, may hold values from -0.29882812 to 0.29882812
- gru_wi: bfloat16 [128, 384], replicated, may hold values from -0.5 to 0.5
- gru_bi: bfloat16 [384], replicated, may hold values from -3 to 3
- gru_wh: bfloat16 [128, 384], replicated, may hold values from -0.5 to 0.5
- gru_bh: bfloat16 [384], replicated, may hold values from -3 to 3
- state_cot: float32 [2, 2048, 128], P(None, 'dp'), may hold values from -6 to 6
Outputs:
- states: float32 [2, 2, 2048, 128], P('section', None, 'dp')
- state_grads: float32 [2, 2, 2048, 128], P('section', None, 'dp')
- grad_edge_w1: float32 [16, 128], replicated
- grad_edge_b1: float32 [128], replicated
- grad_edge_w2: float32 [128, 16384], replicated
- grad_edge_b2: float32 [16384], replicated
- grad_gru_wi: float32 [128, 384], replicated
- grad_gru_bi: float32 [384], replicated
- grad_gru_wh: float32 [128, 384], replicated
- grad_gru_bh: float32 [384], replicated
Inputs may be any that keep to these rules, and one draw needn't show every extreme that they name: `edge_source`: an edge's source and destination lie in the same aligned group of 16 node slots; slot k * (80) onward of a device's edges belong to group k. `edge_target`: same groups as edge_source. `node_labeled`: node 0 of every device's micro-batch is labeled.
All inputs are finite; a program needn't handle non-finite values. No bound on the sum of `edge_valid` on one device may be relied on, other than what follows from the above.
Results may differ from a plain program's by a relative error of at most 0.009.
The roundings to bfloat16 on the way count: a program that leaves them out, or rounds other values in their place, can miss the bound.
Values may be sent and summed in bfloat16 or wider, within the bound.
A program may use at most 128 MiB of HBM per device.

v0:
```python
import jax
import jax.numpy as jnp
from jax import lax
from jax.sharding import PartitionSpec as P

EDGE_BLOCK = 128


def passed_along(value, axis, steps):
    count = lax.axis_size(axis)
    leading, last = (max(0, -steps), min(count, count - steps))
    return lax.ppermute(value, axis, [(source, source + steps) for source in range(leading, last)])


def split_blocks(feats, source, target, valid, block):
    count = feats.shape[1] // block
    return (
        feats.reshape(feats.shape[0], count, block).transpose(1, 0, 2),
        source.reshape(count, block),
        target.reshape(count, block),
        valid.reshape(count, block),
    )


def block_front(feats_b, source_b, weights, state_low):
    width = state_low.shape[1]
    zpre = jnp.dot(feats_b.T, weights[0], preferred_element_type=jnp.float32) + weights[1].astype(
        jnp.float32
    )
    z_low = jax.nn.silu(zpre).astype(jnp.bfloat16)
    amat = (
        jnp.dot(z_low, weights[2], preferred_element_type=jnp.float32)
        + weights[3].astype(jnp.float32)
    ).astype(jnp.bfloat16)
    amat = amat.reshape(-1, width, width)
    node_ids = lax.iota(jnp.int32, state_low.shape[0])
    pick = (source_b[:, None] == node_ids[None, :]).astype(jnp.bfloat16)
    h_source = jnp.dot(pick, state_low, preferred_element_type=jnp.float32).astype(jnp.bfloat16)
    return (zpre, z_low, amat, h_source)


def target_table(target_b, valid_b, nodes):
    node_ids = lax.iota(jnp.int32, nodes)
    return ((target_b[:, None] == node_ids[None, :]) & (valid_b[:, None] > 0)).astype(jnp.bfloat16)


def forward_messages(state_low, blocks, weights):
    nodes, width = state_low.shape

    def add(total, pieces):
        feats_b, source_b, target_b, valid_b = pieces
        _, _, amat, h_source = block_front(feats_b, source_b, weights, state_low)
        message = jnp.einsum("eij,ej->ei", amat, h_source, preferred_element_type=jnp.float32)
        message = message * (valid_b > 0).astype(jnp.float32)[:, None]
        return (total + jax.ops.segment_sum(message, target_b, num_segments=nodes), None)

    summed, _ = lax.scan(add, jnp.zeros((nodes, width), jnp.float32), blocks)
    return summed


def gru_gates(gathered_low, state_low, weights):
    width = state_low.shape[1]
    gate_in = jnp.dot(gathered_low, weights[4], preferred_element_type=jnp.float32) + weights[
        5
    ].astype(jnp.float32)
    gate_state = jnp.dot(state_low, weights[6], preferred_element_type=jnp.float32) + weights[
        7
    ].astype(jnp.float32)
    reset = jax.nn.sigmoid(gate_in[:, :width] + gate_state[:, :width])
    update = jax.nn.sigmoid(gate_in[:, width : 2 * width] + gate_state[:, width : 2 * width])
    candidate = jnp.tanh(gate_in[:, 2 * width :] + reset * gate_state[:, 2 * width :])
    fresh = (1.0 - update) * candidate + update * state_low.astype(jnp.float32)
    return (fresh, gate_state, reset, update, candidate)


def backward_step(upstream, state_low, gathered_low, blocks, weights):
    nodes, width = state_low.shape
    fresh, gate_state, reset, update, candidate = gru_gates(gathered_low, state_low, weights)
    state = state_low.astype(jnp.float32)
    d_cand = upstream * (1.0 - update)
    d_update = upstream * (state - candidate)
    d_state = upstream * update
    d_npre = d_cand * (1.0 - candidate * candidate)
    d_upre = d_update * update * (1.0 - update)
    d_rpre = d_npre * gate_state[:, 2 * width :] * reset * (1.0 - reset)
    d_in = jnp.concatenate([d_rpre, d_upre, d_npre], axis=1).astype(jnp.bfloat16)
    d_hid = jnp.concatenate([d_rpre, d_upre, d_npre * reset], axis=1).astype(jnp.bfloat16)
    grad_wi = jnp.dot(gathered_low.T, d_in, preferred_element_type=jnp.float32)
    grad_bi = jnp.sum(d_in.astype(jnp.float32), axis=0)
    grad_wh = jnp.dot(state_low.T, d_hid, preferred_element_type=jnp.float32)
    grad_bh = jnp.sum(d_hid.astype(jnp.float32), axis=0)
    d_state = d_state + jnp.dot(d_hid, weights[6].T, preferred_element_type=jnp.float32)
    d_gathered = jnp.dot(d_in, weights[4].T, preferred_element_type=jnp.float32).astype(
        jnp.bfloat16
    )

    def back_block(carry, pieces):
        d_src, grad_w1, grad_b1, grad_w2, grad_b2 = carry
        feats_b, source_b, target_b, valid_b = pieces
        zpre, z_low, amat, h_source = block_front(feats_b, source_b, weights, state_low)
        put = target_table(target_b, valid_b, nodes)
        d_msg = jnp.dot(put, d_gathered, preferred_element_type=jnp.float32).astype(jnp.bfloat16)
        d_amat = d_msg.astype(jnp.float32)[:, :, None] * h_source.astype(jnp.float32)[:, None, :]
        d_amat = d_amat.reshape(d_amat.shape[0], width * width).astype(jnp.bfloat16)
        grad_w2 = grad_w2 + jnp.dot(z_low.T, d_amat, preferred_element_type=jnp.float32)
        grad_b2 = grad_b2 + jnp.sum(d_amat.astype(jnp.float32), axis=0)
        d_z = jnp.dot(d_amat, weights[2].T, preferred_element_type=jnp.float32)
        sig = jax.nn.sigmoid(zpre)
        d_zpre = (d_z * sig * (1.0 + zpre * (1.0 - sig))).astype(jnp.bfloat16)
        grad_w1 = grad_w1 + jnp.dot(feats_b, d_zpre, preferred_element_type=jnp.float32)
        grad_b1 = grad_b1 + jnp.sum(d_zpre.astype(jnp.float32), axis=0)
        d_source = jnp.einsum("eij,ei->ej", amat, d_msg, preferred_element_type=jnp.float32)
        d_src = d_src + jax.ops.segment_sum(d_source, source_b, num_segments=nodes)
        return ((d_src, grad_w1, grad_b1, grad_w2, grad_b2), None)

    start = (
        jnp.zeros((nodes, width), jnp.float32),
        jnp.zeros(weights[0].shape, jnp.float32),
        jnp.zeros(weights[1].shape, jnp.float32),
        jnp.zeros(weights[2].shape, jnp.float32),
        jnp.zeros(weights[3].shape, jnp.float32),
    )
    ends, _ = lax.scan(back_block, start, blocks)
    d_total = d_state + ends[0]
    return (d_total, (ends[1], ends[2], ends[3], ends[4], grad_wi, grad_bi, grad_wh, grad_bh))


def shards(
    node_input,
    edge_input,
    edge_source,
    edge_target,
    edge_valid,
    node_labeled,
    edge_w1,
    edge_b1,
    edge_w2,
    edge_b2,
    gru_wi,
    gru_bi,
    gru_wh,
    gru_bh,
    state_cot,
):
    weights = (edge_w1, edge_b1, edge_w2, edge_b2, gru_wi, gru_bi, gru_wh, gru_bh)
    micro, nodes, width = node_input.shape
    block = min(EDGE_BLOCK, edge_input.shape[2])
    section_id = lax.axis_index("section")
    first = section_id == 0
    count_local = jnp.sum(node_labeled.astype(jnp.float32))

    def batch_blocks(index):
        feats = lax.dynamic_index_in_dim(edge_input, index, 0, keepdims=False)
        source = lax.dynamic_index_in_dim(edge_source, index, 0, keepdims=False)
        target = lax.dynamic_index_in_dim(edge_target, index, 0, keepdims=False)
        valid = lax.dynamic_index_in_dim(edge_valid, index, 0, keepdims=False)
        return split_blocks(feats, source, target, valid, block)

    received = jnp.zeros((nodes, width), jnp.bfloat16)
    saved = []
    states_out = jnp.zeros((micro, nodes, width), jnp.float32)
    for tick in range(micro + 1):
        batch = tick - section_id
        live = (batch >= 0) & (batch < micro)
        index = jnp.clip(batch, 0, micro - 1)
        state_low = jnp.where(first, node_input[min(tick, micro - 1)], received)
        blocks = batch_blocks(index)
        gathered_low = forward_messages(state_low, blocks, weights).astype(jnp.bfloat16)
        fresh = gru_gates(gathered_low, state_low, weights)[0]
        saved.append((state_low, gathered_low))
        sending = fresh.astype(jnp.bfloat16)
        value = jnp.where(first, sending.astype(jnp.float32), fresh)
        states_out = jnp.where(
            live, lax.dynamic_update_index_in_dim(states_out, value, index, 0), states_out
        )
        if tick < micro:
            received = passed_along(sending, "section", 1)
    grad_received = jnp.zeros((nodes, width), jnp.bfloat16)
    grads_out = jnp.zeros((micro, nodes, width), jnp.float32)
    totals = tuple((jnp.zeros(w.shape, jnp.float32) for w in weights))
    for tick in range(micro + 1):
        batch = micro - tick - section_id
        live = (batch >= 0) & (batch < micro)
        index = jnp.clip(batch, 0, micro - 1)
        state_low, gathered_low = saved[micro - tick]
        labels = lax.dynamic_index_in_dim(node_labeled, index, 0, keepdims=False).astype(
            jnp.float32
        )
        top = lax.dynamic_index_in_dim(state_cot, index, 0, keepdims=False) * labels[:, None]
        upstream = jnp.where(first, grad_received.astype(jnp.float32), top)
        d_total, terms = backward_step(
            upstream, state_low, gathered_low, batch_blocks(index), weights
        )
        totals = tuple((acc + jnp.where(live, term, 0.0) for acc, term in zip(totals, terms)))
        sending = d_total.astype(jnp.bfloat16)
        value = jnp.where(first, d_total, sending.astype(jnp.float32))
        grads_out = jnp.where(
            live, lax.dynamic_update_index_in_dim(grads_out, value, index, 0), grads_out
        )
        if tick < micro:
            grad_received = passed_along(sending, "section", -1)
    count_total = lax.psum(count_local, "dp")
    summed = lax.psum(
        (totals[0], totals[1], totals[2], totals[3], totals[4], totals[5], totals[6], totals[7]),
        ("section", "dp"),
    )
    scaled = [g / count_total for g in summed]
    return (
        states_out[None],
        grads_out[None],
        scaled[0],
        scaled[1],
        scaled[2],
        scaled[3],
        scaled[4],
        scaled[5],
        scaled[6],
        scaled[7],
    )


def solution(mesh):
    placed = (
        P(None, "dp", None),
        P(None, None, "dp"),
        P(None, "dp"),
        P(None, "dp"),
        P(None, "dp"),
        P(None, "dp"),
        P(),
        P(),
        P(),
        P(),
        P(),
        P(),
        P(),
        P(),
        P(None, "dp", None),
    )
    return jax.shard_map(
        shards,
        mesh=mesh,
        in_specs=placed,
        out_specs=(
            P("section", None, "dp", None),
            P("section", None, "dp", None),
            P(),
            P(),
            P(),
            P(),
            P(),
            P(),
            P(),
            P(),
        ),
        check_vma=False,
    )
```

profile of v0, /device:TPU:0, one launch (start us, length us, event | category | flops | bytes accessed | tf_op | source)
XLA Modules:
  0.0 941.3 jit_solution(15465761410084923599)
XLA Ops:
  12.0 71.9 %while.87 = (s32[]{:T(128)}, f32[128,128]{1,0:T(8,128)S(1)}, s32[5,128]{1,0:T(8,128)S(1)}, bf16[5,16,128]{2,1,0:T(8,128)(2,1)S(1)}, bf16[16,128]{1,0:T(8,128)(2,...) while((s32[]{:T(128)}, f32[128,128]{1,0:T(8,128)S(1)}, ...), condition=%wide.region_2.3_spmd, body=%wide.region_0.2_spmd.sunk | while | flops 550158720 | bytes 21443976 | solution.py:57
  13.5 5.6 fusion.396
  27.8 5.6 fusion.396
  42.2 5.6 fusion.396
  56.6 5.6 fusion.396
  71.0 5.6 fusion.396
  89.1 71.9 %while.88 = (s32[]{:T(128)}, f32[128,128]{1,0:T(8,128)S(1)}, s32[5,128]{1,0:T(8,128)S(1)}, bf16[5,16,128]{2,1,0:T(8,128)(2,1)S(1)}, bf16[16,128]{1,0:T(8,128)(2,...) while((s32[]{:T(128)}, f32[128,128]{1,0:T(8,128)S(1)}, ...), condition=%wide.region_5.6_spmd, body=%wide.region_3.5_spmd.sunk | while | flops 550158720 | bytes 21443976 | solution.py:57
  90.5 5.6 fusion.408
  104.9 5.6 fusion.408
  119.3 5.6 fusion.408
  133.7 5.6 fusion.408
  148.1 5.6 fusion.408
  164.8 71.6 %while.89 = (s32[]{:T(128)}, f32[128,128]{1,0:T(8,128)S(1)}, s32[5,128]{1,0:T(8,128)S(1)}, bf16[5,16,128]{2,1,0:T(8,128)(2,1)S(1)}, bf16[16,128]{1,0:T(8,128)(2,...) while((s32[]{:T(128)}, f32[128,128]{1,0:T(8,128)S(1)}, ...), condition=%wide.region_8.9_spmd, body=%wide.region_6.8_spmd.sunk | while | flops 550158720 | bytes 21443976 | solution.py:57
  166.3 5.6 fusion.420
  180.6 5.6 fusion.420
  194.9 5.6 fusion.420
  209.2 5.6 fusion.420
  223.5 5.6 fusion.420
  237.3 160.5 %while.90 = (s32[]{:T(128)}, f32[128,128]{1,0:T(8,128)S(1)}, f32[16,128]{1,0:T(8,128)S(1)}, f32[128]{0:T(128)S(1)}, f32[128,16384]{1,0:T(8,128)}, /*index=5*/f32...) while((s32[]{:T(128)}, f32[128,128]{1,0:T(8,128)S(1)}, ...), condition=%wide.region_13.14_spmd.clone, body=%wide.region_9.13_spmd.clone.sunk | while | flops 1641550208 | bytes 89526008 | solution.py:123
  247.2 4.9 convert_reduce_fusion.19
  256.6 9.0 convolution_add_fusion.36
  275.6 4.9 convert_reduce_fusion.19
  284.9 11.5 %convolution_add_fusion.36 = f32[128,16384]{1,0:T(8,128)} fusion(f32[128,16384]{1,0:T(8,128)} %get-tuple-element.1704, pred[]{:T(512)S(6)} %compare.9, bf16[16,8,128,128]{3,2,1,0:T(8,128)(2,1)} %bitcast.476, f32[128,128]{1,0:T(8,128)S(1)} %convolution_add_fusion.34), kind=kOutput, calls=%fused_computation.87.clone.1 | convolution fusion | flops 541147136 | bytes 21037056 | tf_op jit(solution)/shard_map/while/body/eval_jaxpr/dot_general | solution.py:105
  306.3 4.9 convert_reduce_fusion.19
  315.7 11.5 %convolution_add_fusion.36 = f32[128,16384]{1,0:T(8,128)} fusion(f32[128,16384]{1,0:T(8,128)} %get-tuple-element.1704, pred[]{:T(512)S(6)} %compare.9, bf16[16,8,128,128]{3,2,1,0:T(8,128)(2,1)} %bitcast.476, f32[128,128]{1,0:T(8,128)S(1)} %convolution_add_fusion.34), kind=kOutput, calls=%fused_computation.87.clone.1 | convolution fusion | flops 541147136 | bytes 21037056 | tf_op jit(solution)/shard_map/while/body/eval_jaxpr/dot_general | solution.py:105
  346.5 11.5 %convolution_add_fusion.36 = f32[128,16384]{1,0:T(8,128)} fusion(f32[128,16384]{1,0:T(8,128)} %get-tuple-element.1704, pred[]{:T(512)S(6)} %compare.9, bf16[16,8,128,128]{3,2,1,0:T(8,128)(2,1)} %bitcast.476, f32[128,128]{1,0:T(8,128)S(1)} %convolution_add_fusion.34), kind=kOutput, calls=%fused_computation.87.clone.1 | convolution fusion | flops 541147136 | bytes 21037056 | tf_op jit(solution)/shard_map/while/body/eval_jaxpr/dot_general | solution.py:105
  377.2 11.5 %convolution_add_fusion.36 = f32[128,16384]{1,0:T(8,128)} fusion(f32[128,16384]{1,0:T(8,128)} %get-tuple-element.1704, pred[]{:T(512)S(6)} %compare.9, bf16[16,8,128,128]{3,2,1,0:T(8,128)(2,1)} %bitcast.476, f32[128,128]{1,0:T(8,128)S(1)} %convolution_add_fusion.34), kind=kOutput, calls=%fused_computation.87.clone.1 | convolution fusion | flops 541147136 | bytes 21037056 | tf_op jit(solution)/shard_map/while/body/eval_jaxpr/dot_general | solution.py:105
  401.7 152.6 %while.91 = (s32[]{:T(128)}, f32[128,128]{1,0:T(8,128)S(1)}, f32[16,128]{1,0:T(8,128)S(1)}, f32[128]{0:T(128)S(1)}, f32[128,16384]{1,0:T(8,128)}, /*index=5*/f32...) while((s32[]{:T(128)}, f32[128,128]{1,0:T(8,128)S(1)}, ...), condition=%wide.region_18.19_spmd.clone, body=%wide.region_14.18_spmd.clone.sunk | while | flops 1641550208 | bytes 89526008 | solution.py:123
  411.8 4.9 convert_reduce_fusion.21
  421.2 9.2 convolution_add_fusion.39
  449.6 11.6 %convolution_add_fusion.39 = f32[128,16384]{1,0:T(8,128)} fusion(f32[128,16384]{1,0:T(8,128)} %get-tuple-element.1758, pred[]{:T(512)S(6)} %compare.10, bf16[16,8,128,128]{3,2,1,0:T(8,128)(2,1)} %bitcast.478, f32[128,128]{1,0:T(8,128)S(1)} %convolution_add_fusion.37), kind=kOutput, calls=%fused_computation.132.clone.1 | convolution fusion | flops 541147136 | bytes 21037056 | tf_op jit(solution)/shard_map/while/body/eval_jaxpr/dot_general | solution.py:105
  471.2 4.9 convert_reduce_fusion.21
  480.6 11.6 %convolution_add_fusion.39 = f32[128,16384]{1,0:T(8,128)} fusion(f32[128,16384]{1,0:T(8,128)} %get-tuple-element.1758, pred[]{:T(512)S(6)} %compare.10, bf16[16,8,128,128]{3,2,1,0:T(8,128)(2,1)} %bitcast.478, f32[128,128]{1,0:T(8,128)S(1)} %convolution_add_fusion.37), kind=kOutput, calls=%fused_computation.132.clone.1 | convolution fusion | flops 541147136 | bytes 21037056 | tf_op jit(solution)/shard_map/while/body/eval_jaxpr/dot_general | solution.py:105
  502.2 4.9 convert_reduce_fusion.21
  511.5 11.6 %convolution_add_fusion.39 = f32[128,16384]{1,0:T(8,128)} fusion(f32[128,16384]{1,0:T(8,128)} %get-tuple-element.1758, pred[]{:T(512)S(6)} %compare.10, bf16[16,8,128,128]{3,2,1,0:T(8,128)(2,1)} %bitcast.478, f32[128,128]{1,0:T(8,128)S(1)} %convolution_add_fusion.37), kind=kOutput, calls=%fused_computation.132.clone.1 | convolution fusion | flops 541147136 | bytes 21037056 | tf_op jit(solution)/shard_map/while/body/eval_jaxpr/dot_general | solution.py:105
  542.5 11.6 %convolution_add_fusion.39 = f32[128,16384]{1,0:T(8,128)} fusion(f32[128,16384]{1,0:T(8,128)} %get-tuple-element.1758, pred[]{:T(512)S(6)} %compare.10, bf16[16,8,128,128]{3,2,1,0:T(8,128)(2,1)} %bitcast.478, f32[128,128]{1,0:T(8,128)S(1)} %convolution_add_fusion.37), kind=kOutput, calls=%fused_computation.132.clone.1 | convolution fusion | flops 541147136 | bytes 21037056 | tf_op jit(solution)/shard_map/while/body/eval_jaxpr/dot_general | solution.py:105
  558.2 161.8 %while.92 = (s32[]{:T(128)}, f32[128,128]{1,0:T(8,128)S(1)}, f32[16,128]{1,0:T(8,128)S(1)}, f32[128]{0:T(128)S(1)}, f32[128,16384]{1,0:T(8,128)}, /*index=5*/f32...) while((s32[]{:T(128)}, f32[128,128]{1,0:T(8,128)S(1)}, ...), condition=%wide.region_23.24_spmd.clone, body=%wide.region_19.23_spmd.clone.sunk | while | flops 1641550208 | bytes 89526008 | solution.py:123
  569.6 4.9 convert_reduce_fusion.23
  579.6 9.0 convolution_add_fusion.42
  609.9 11.4 %convolution_add_fusion.42 = f32[128,16384]{1,0:T(8,128)} fusion(f32[128,16384]{1,0:T(8,128)} %get-tuple-element.1812, pred[]{:T(512)S(6)} %compare.11, bf16[16,8,128,128]{3,2,1,0:T(8,128)(2,1)} %bitcast.480, f32[128,128]{1,0:T(8,128)S(1)} %convolution_add_fusion.40), kind=kOutput, calls=%fused_computation.177.clone.1 | convolution fusion | flops 541147136 | bytes 21037056 | tf_op jit(solution)/shard_map/while/body/eval_jaxpr/dot_general | solution.py:105
  642.7 11.4 %convolution_add_fusion.42 = f32[128,16384]{1,0:T(8,128)} fusion(f32[128,16384]{1,0:T(8,128)} %get-tuple-element.1812, pred[]{:T(512)S(6)} %compare.11, bf16[16,8,128,128]{3,2,1,0:T(8,128)(2,1)} %bitcast.480, f32[128,128]{1,0:T(8,128)S(1)} %convolution_add_fusion.40), kind=kOutput, calls=%fused_computation.177.clone.1 | convolution fusion | flops 541147136 | bytes 21037056 | tf_op jit(solution)/shard_map/while/body/eval_jaxpr/dot_general | solution.py:105
  675.5 11.4 %convolution_add_fusion.42 = f32[128,16384]{1,0:T(8,128)} fusion(f32[128,16384]{1,0:T(8,128)} %get-tuple-element.1812, pred[]{:T(512)S(6)} %compare.11, bf16[16,8,128,128]{3,2,1,0:T(8,128)(2,1)} %bitcast.480, f32[128,128]{1,0:T(8,128)S(1)} %convolution_add_fusion.40), kind=kOutput, calls=%fused_computation.177.clone.1 | convolution fusion | flops 541147136 | bytes 21037056 | tf_op jit(solution)/shard_map/while/body/eval_jaxpr/dot_general | solution.py:105
  708.3 11.4 %convolution_add_fusion.42 = f32[128,16384]{1,0:T(8,128)} fusion(f32[128,16384]{1,0:T(8,128)} %get-tuple-element.1812, pred[]{:T(512)S(6)} %compare.11, bf16[16,8,128,128]{3,2,1,0:T(8,128)(2,1)} %bitcast.480, f32[128,128]{1,0:T(8,128)S(1)} %convolution_add_fusion.40), kind=kOutput, calls=%fused_computation.177.clone.1 | convolution fusion | flops 541147136 | bytes 21037056 | tf_op jit(solution)/shard_map/while/body/eval_jaxpr/dot_general | solution.py:105
  722.1 10.1 %select_add_fusion = f32[128,16384]{1,0:T(8,128)} fusion(f32[128,16384]{1,0:T(8,128)} %get-tuple-element.453, f32[128,16384]{1,0:T(8,128)} %get-tuple-element.452, f32[128,16384]{1,0:T(8,128)} %get-tuple-element.451, pred[]{:T(512)S(6)} %and.37, pred[]{:T(512)S(6)} %and.38, pred[]{:T(512)S(6)} %and.39), kind=kLoop, calls=%fused_computation.222 | loop fusion | flops 10485760 | bytes 33554436 | tf_op jit(solution)/shard_map/add | solution.py:194
  734.1 45.2 %psum.64 = f32[]{:T(128)} all-reduce(f32[]{:T(128)} %convert_reduce_fusion.12), channel_id=1, replica_groups=mesh['section'=2,'dp'=16] {'dp'}, use_global_device_ids=true, to_apply=%region_26.27 | all-reduce | flops 1 | bytes 8 | tf_op jit(solution)/shard_map/psum | solution.py:202
  779.7 37.6 %all-reduce = (f32[16,128]{1,0:T(8,128)S(1)}, f32[128]{0:T(128)S(1)}, f32[384]{0:T(512)S(1)}, f32[384]{0:T(512)S(1)}) all-reduce(f32[16,128]{1,0:T(8,128)S(1)} %select_add_fusion.2, f32[128]{0:T(128)S(1)} %fusion.232, f32[384]{0:T(512)S(1)} %select_add_fusion.4, ...), channel_id=1, replica_groups=mesh['section'=2,'dp'=16] {'section','dp'}, use_global_device_ids=true, to_apply=%region_24.25 | all-reduce | flops 2944 | bytes 23552 | tf_op jit(solution)/shard_map/psum | solution.py:203
  822.3 99.5 %all-reduce.4.cloned.1.call-done = (f32[128,16384]{1,0:T(8,128)}, f32[16384]{0:T(1024)}, f32[128,384]{1,0:T(8,128)}, f32[128,384]{1,0:T(8,128)}) async-done(((f32[128,16384]{1,0:T(8,128)}, f32[16384]{0:T(1024)}, f32[128,384]{1,0:T(8,128)}, f32[128,384]{1,0:T(8,128)}), (f32[128,16384]{1,0:T(8,128)}, f32[16384]{0:T(1024)}, f32[128,384]{1,0:T(8,128)}, f32[128,384]{1,0:T(8,128)})) %all-reduce.4.cloned.1.call-update) | async-done | bytes 8847376 | tf_op jit(solution)/shard_map/psum | solution.py:203
  921.8 8.3 broadcast_divide_fusion
  (615 shorter events, 429.5 us)
Async XLA Ops:
  7.2 76.8 %copy-start = (bf16[128,384]{1,0:T(8,128)(2,1)S(1)}, bf16[128,384]{1,0:T(8,128)(2,1)}, u32[]{:S(2)}) copy-start(bf16[128,384]{1,0:T(8,128)(2,1)} %param.39) | copy-start | bytes 294916
  7.2 914.6 %all-reduce.4.cloned.1.call-start = ((), (), s32[]{:S(2)}) async-start(), calls=%async_computation | async-start | bytes 17694720 | tf_op jit(solution)/shard_map/psum | solution.py:203
  12.0 72.2 %copy-start.18 = (bf16[128,384]{1,0:T(8,128)(2,1)S(1)}, bf16[128,384]{1,0:T(8,128)(2,1)}, u32[]{:S(2)}) copy-start(bf16[128,384]{1,0:T(8,128)(2,1)} %param.37) | copy-start | bytes 294916
  12.0 72.9 %copy-start.26 = (bf16[2,128,128]{2,1,0:T(8,128)(2,1)S(1)}, bf16[2,128,128]{2,1,0:T(8,128)(2,1)}, u32[]{:S(2)}) copy-start(bf16[2,128,128]{2,1,0:T(8,128)(2,1)} %param.27) | copy-start | bytes 196612
  85.6 3.2 collective-permute-start
  89.0 74.8 %copy-start.57 = (s32[2,128]{1,0:T(2,128)S(1)}, s32[2,128]{1,0:T(2,128)}, u32[]{:S(2)}) copy-start(s32[2,128]{1,0:T(2,128)} %param.32) | copy-start | bytes 3076
  161.3 239.9 %copy-start.20 = (f32[128,128]{1,0:T(8,128)}, f32[128,128]{1,0:T(8,128)S(1)}, u32[]{:S(2)}) copy-start(f32[128,128]{1,0:T(8,128)S(1)} %get-tuple-element.970) | copy-start | bytes 196612
  161.3 3.2 collective-permute-start.1
  164.8 71.8 %copy-start.19 = (f32[2,128,128]{2,1,0:T(8,128)S(1)}, f32[2,128,128]{2,1,0:T(8,128)}, u32[]{:S(2)}) copy-start(f32[2,128,128]{2,1,0:T(8,128)} %param.41) | copy-start | bytes 393220
  236.7 161.2 %copy-start.30 = (f32[128,128]{1,0:T(8,128)}, f32[128,128]{1,0:T(8,128)S(1)}, u32[]{:S(2)}) copy-start(f32[128,128]{1,0:T(8,128)S(1)} %get-tuple-element.968) | copy-start | bytes 196612
  236.7 161.2 %copy-start.39 = (bf16[128,128]{1,0:T(8,128)(2,1)}, bf16[128,128]{1,0:T(8,128)(2,1)S(1)}, u32[]{:S(2)}) copy-start(bf16[128,128]{1,0:T(8,128)(2,1)S(1)} %get-tuple-element.965) | copy-start | bytes 98308
  236.8 162.6 %copy-start.34 = (bf16[128,128]{1,0:T(8,128)(2,1)}, bf16[128,128]{1,0:T(8,128)(2,1)S(1)}, u32[]{:S(2)}) copy-start(bf16[128,128]{1,0:T(8,128)(2,1)S(1)} %get-tuple-element.1011) | copy-start | bytes 98308
  236.8 162.6 %copy-start.41 = (bf16[128,128]{1,0:T(8,128)(2,1)}, bf16[128,128]{1,0:T(8,128)(2,1)S(1)}, u32[]{:S(2)}) copy-start(bf16[128,128]{1,0:T(8,128)(2,1)S(1)} %get-tuple-element.1012) | copy-start | bytes 98308
  236.9 162.5 %copy-start.36 = (bf16[128,128]{1,0:T(8,128)(2,1)}, bf16[128,128]{1,0:T(8,128)(2,1)S(1)}, u32[]{:S(2)}) copy-start(bf16[128,128]{1,0:T(8,128)(2,1)S(1)} %fusion.180) | copy-start | bytes 98308
  398.1 3.1 collective-permute-start.2
  401.6 154.4 %copy-start.25 = (f32[128,128]{1,0:T(8,128)S(1)}, f32[128,128]{1,0:T(8,128)}, u32[]{:S(2)}) copy-start(f32[128,128]{1,0:T(8,128)} %copy-done.24) | copy-start | bytes 196612
  401.6 156.2 %copy-start.15 = (f32[128,384]{1,0:T(8,128)S(1)}, f32[128,384]{1,0:T(8,128)}, u32[]{:S(2)}) copy-start(f32[128,384]{1,0:T(8,128)} %copy-done.14) | copy-start | bytes 589828
  401.6 156.2 %copy-start.17 = (f32[128,384]{1,0:T(8,128)S(1)}, f32[128,384]{1,0:T(8,128)}, u32[]{:S(2)}) copy-start(f32[128,384]{1,0:T(8,128)} %copy-done.16) | copy-start | bytes 589828
  401.6 156.1 %copy-start.27 = (bf16[2,128,128]{2,1,0:T(8,128)(2,1)S(1)}, bf16[2,128,128]{2,1,0:T(8,128)(2,1)}, u32[]{:S(2)}) copy-start(bf16[2,128,128]{2,1,0:T(8,128)(2,1)} %param.27) | copy-start | bytes 196612
  401.6 156.1 %copy-start.32 = (f32[128,128]{1,0:T(8,128)S(1)}, f32[128,128]{1,0:T(8,128)}, u32[]{:S(2)}) copy-start(f32[128,128]{1,0:T(8,128)} %get-tuple-element.974) | copy-start | bytes 196612
  401.6 156.1 %copy-start.33 = (f32[128,128]{1,0:T(8,128)S(1)}, f32[128,128]{1,0:T(8,128)}, u32[]{:S(2)}) copy-start(f32[128,128]{1,0:T(8,128)} %get-tuple-element.973) | copy-start | bytes 196612
  401.6 156.1 %copy-start.59 = (f32[128]{0:T(128)S(1)}, f32[128]{0:T(128)}, u32[]{:S(2)}) copy-start(f32[128]{0:T(128)} %get-tuple-element.1016) | copy-start | bytes 1540
  401.6 156.5 %copy-start.10 = (bf16[128,128]{1,0:T(8,128)(2,1)S(1)}, bf16[128,128]{1,0:T(8,128)(2,1)}, u32[]{:S(2)}) copy-start(bf16[128,128]{1,0:T(8,128)(2,1)} %copy-done.9) | copy-start | bytes 98308
  401.7 156.5 %copy-start.11 = (f32[16384]{0:T(1024)S(1)}, f32[16384]{0:T(1024)}, u32[]{:S(2)}) copy-start(f32[16384]{0:T(1024)} %custom-call.11) | copy-start | bytes 196612
  401.7 156.5 %copy-start.43 = (f32[16,128]{1,0:T(8,128)S(1)}, f32[16,128]{1,0:T(8,128)}, u32[]{:S(2)}) copy-start(f32[16,128]{1,0:T(8,128)} %custom-call.8) | copy-start | bytes 24580
  401.7 156.5 %copy-start.53 = (f32[128]{0:T(128)S(1)}, f32[128]{0:T(128)}, u32[]{:S(2)}) copy-start(f32[128]{0:T(128)} %custom-call.9) | copy-start | bytes 1540
  411.6 5.1 copy-start.2
  471.0 5.1 copy-start.2
  502.0 5.1 copy-start.2
  554.6 3.1 collective-permute-start.3
  558.2 161.9 %copy-start.23 = (f32[128,128]{1,0:T(8,128)S(1)}, f32[128,128]{1,0:T(8,128)}, u32[]{:S(2)}) copy-start(f32[128,128]{1,0:T(8,128)} %copy-done.22) | copy-start | bytes 196612
  558.2 163.0 %copy-start.8 = (bf16[128,128]{1,0:T(8,128)(2,1)S(1)}, bf16[128,128]{1,0:T(8,128)(2,1)}, u32[]{:S(2)}) copy-start(bf16[128,128]{1,0:T(8,128)(2,1)} %copy-done.7) | copy-start | bytes 98308
  558.2 163.0 %copy-start.35 = (bf16[128,128]{1,0:T(8,128)(2,1)S(1)}, bf16[128,128]{1,0:T(8,128)(2,1)}, u32[]{:S(2)}) copy-start(bf16[128,128]{1,0:T(8,128)(2,1)} %copy-done.34) | copy-start | bytes 98308
  558.2 163.0 %copy-start.37 = (bf16[128,128]{1,0:T(8,128)(2,1)S(1)}, bf16[128,128]{1,0:T(8,128)(2,1)}, u32[]{:S(2)}) copy-start(bf16[128,128]{1,0:T(8,128)(2,1)} %copy-done.36) | copy-start | bytes 98308
  558.2 163.0 %copy-start.40 = (bf16[128,128]{1,0:T(8,128)(2,1)S(1)}, bf16[128,128]{1,0:T(8,128)(2,1)}, u32[]{:S(2)}) copy-start(bf16[128,128]{1,0:T(8,128)(2,1)} %copy-done.39) | copy-start | bytes 98308
  569.4 5.1 copy-start.3
  722.1 10.1 %copy-start.13 = (f32[16384]{0:T(1024)S(1)}, f32[16384]{0:T(1024)}, u32[]{:S(2)}) copy-start(f32[16384]{0:T(1024)} %copy-done.12) | copy-start | bytes 196612
  732.8 46.5 %copy-start.21 = (f32[128,128]{1,0:T(8,128)S(1)}, f32[128,128]{1,0:T(8,128)}, u32[]{:S(2)}) copy-start(f32[128,128]{1,0:T(8,128)} %copy-done.20) | copy-start | bytes 196612
  732.8 46.6 %copy-start.42 = (bf16[128,128]{1,0:T(8,128)(2,1)S(1)}, bf16[128,128]{1,0:T(8,128)(2,1)}, u32[]{:S(2)}) copy-start(bf16[128,128]{1,0:T(8,128)(2,1)} %copy-done.41) | copy-start | bytes 98308
  732.8 46.7 %copy-start.29 = (f32[128,128]{1,0:T(8,128)S(1)}, f32[128,128]{1,0:T(8,128)}, u32[]{:S(2)}) copy-start(f32[128,128]{1,0:T(8,128)} %copy-done.28) | copy-start | bytes 196612
  732.8 46.7 %copy-start.31 = (f32[128,128]{1,0:T(8,128)S(1)}, f32[128,128]{1,0:T(8,128)}, u32[]{:S(2)}) copy-start(f32[128,128]{1,0:T(8,128)} %copy-done.30) | copy-start | bytes 196612
  732.9 46.8 %copy-start.55 = (f32[128]{0:T(128)S(1)}, f32[128]{0:T(128)}, u32[]{:S(2)}) copy-start(f32[128]{0:T(128)} %copy-done.54) | copy-start | bytes 1540
  732.9 46.8 %copy-start.45 = (f32[16,128]{1,0:T(8,128)S(1)}, f32[16,128]{1,0:T(8,128)}, u32[]{:S(2)}) copy-start(f32[16,128]{1,0:T(8,128)} %copy-done.44) | copy-start | bytes 24580
  779.5 150.6 %copy-start.49 = (f32[1,2,128,128]{3,2,1,0:T(8,128)}, f32[1,2,128,128]{3,2,1,0:T(8,128)S(1)}, u32[]{:S(2)}) copy-start(f32[1,2,128,128]{3,2,1,0:T(8,128)S(1)} %bitcast_dynamic-update-slice_fusion.2) | copy-start | bytes 393220
  822.3 107.8 %copy-start.48 = (f32[1,2,128,128]{3,2,1,0:T(8,128)}, f32[1,2,128,128]{3,2,1,0:T(8,128)S(1)}, u32[]{:S(2)}) copy-start(f32[1,2,128,128]{3,2,1,0:T(8,128)S(1)} %bitcast_dynamic-update-slice_fusion) | copy-start | bytes 393220
  921.8 8.3 copy-start.50
  921.8 9.5 %copy-start.47 = (f32[128,384]{1,0:T(8,128)S(1)}, f32[128,384]{1,0:T(8,128)}, u32[]{:S(2)}) copy-start(f32[128,384]{1,0:T(8,128)} %get-tuple-element.955) | copy-start | bytes 589828
  921.8 10.9 %copy-start.46 = (f32[128,384]{1,0:T(8,128)S(1)}, f32[128,384]{1,0:T(8,128)}, u32[]{:S(2)}) copy-start(f32[128,384]{1,0:T(8,128)} %get-tuple-element.956) | copy-start | bytes 589828
  (41 other events, 171.4 us)
Sparse Core Ops, SparseCore 0:
  733.0 188.7 all-reduce.3
where the time goes:
time: 953 us; the launch traced here: 941 us
  matrix products  449 us (47%)
  other arithmetic  193 us (20%)
  waiting for transfers between devices  103 us (11%)
  blocking collectives  82.8 us (9%)
  local copies, waits for them, and re-layouts  78 us (8%)
  between operations  15.7 us (2%)
  loops' own time  11.8 us (1%)
    dot_general x15, matrix products, back_block(): jnp.dot(z_low.T, d_amat, preferred_element_type=jnp.float32)  165 us
    dot_general x30, matrix products, block_front(): jnp.dot(z_low, weights[2], preferred_element_type=jnp.float32)  136 us
    psum x1, waiting for transfers between devices, shards(): lax.psum((totals[0], totals[1], totals[2], totals[3], totals[4], totals[5...  99.5 us
    reduce_sum x15, other arithmetic, back_block(): grad_b2 = grad_b2 + jnp.sum(d_amat.astype(jnp.float32), axis=0)  73.3 us
    while x90, local copies, waits for them, and re-layouts  70 us
    dot_general x15, matrix products, back_block(): d_z = jnp.dot(d_amat, weights[2].T, preferred_element_type=jnp.float32)  64 us
    psum x1, blocking collectives, shards(): count_total = lax.psum(count_local, 'dp')  45.2 us
    psum x1, blocking collectives, shards(): lax.psum((totals[0], totals[1], totals[2], totals[3], totals[4], totals[5...  37.6 us
  transfers between devices with their start and end apart: 5, of which 4 were waited for; matrix products, arithmetic and copies ran while one was open for 1% of the time, Pallas kernels for 0%

commit v1 on v0

--- a/solution.py
+++ b/solution.py
@@ -1,7 +1,403 @@
+import functools
+
 import jax
 import jax.numpy as jnp
 from jax import lax
+from jax.experimental import pallas as pl
+from jax.experimental.pallas import tpu as pltpu
 from jax.sharding import PartitionSpec as P
+
+BF, F32 = jnp.bfloat16, jnp.float32
+VMEM = pltpu.VMEM
+LANE = 128
+ROUND = 16
+SMALL_ROWS = 1024
+
+
+def dot(a, b, ca=1, cb=0):
+    return lax.dot_general(a, b, (((ca,), (cb,)), ((), ())), preferred_element_type=F32)
+
+
+def split(x, parts):
+    out = []
+    for _ in range(parts - 1):
+        piece = x.astype(BF)
+        out.append(piece)
+        x = x - piece.astype(F32)
+    out.append(x.astype(BF))
+    return out
+
+
+def loop(count, body):
+    def step(i, carry):
+        body(i)
+        return carry
+
+    lax.fori_loop(0, count, step, 0)
+
+
+def aligned(i, size):
+    return pl.ds(pl.multiple_of(i * size, size), size)
+
+
+def edge_tables(ends, nodes):
+    ids = lax.broadcasted_iota(jnp.int32, (nodes, ends.shape[1]), 0).astype(F32)
+    pick = (ids == ends[0:1]).astype(F32).astype(BF)
+    put = (ids == ends[1:2]).astype(F32).astype(BF)
+    return pick, put
+
+
+def pack_ends(src_ref, tgt_ref, valid_ref, lab_ref, s):
+    row = pl.ds(s, 1)
+    src = src_ref[row, :].astype(F32)
+    tgt = jnp.where(valid_ref[row, :] > 0, tgt_ref[row, :], -1).astype(F32)
+    lab = lab_ref[row, :].astype(F32)
+    edges, nodes = src.shape[1], lab.shape[1]
+    lab = jnp.concatenate([lab, jnp.zeros((1, edges - nodes), F32)], axis=1)
+    return jnp.concatenate([src, tgt, lab, jnp.zeros((13, edges), F32)], axis=0)
+
+
+def edge_hidden(feats, w1, b1):
+    bias = jnp.broadcast_to(b1.astype(F32), (LANE, LANE)).T[:, 0:1]
+    return dot(w1, feats, 0, 0) + bias
+
+
+def gru_forward(m, h, wi, bi, wh, bh):
+    w = h.shape[1]
+    gi = dot(m, wi) + bi.astype(F32)
+    gh = dot(h, wh) + bh.astype(F32)
+    r = jax.nn.sigmoid(gi[:, :w] + gh[:, :w])
+    u = jax.nn.sigmoid(gi[:, w : 2 * w] + gh[:, w : 2 * w])
+    n = jnp.tanh(gi[:, 2 * w :] + r * gh[:, 2 * w :])
+    fresh = (1.0 - u) * n + u * h.astype(F32)
+    return fresh, gh[:, 2 * w :], r, u, n
+
+
+def gru_backward(g, h, gates, wi, wh):
+    _, ghn, r, u, n = gates
+    dn = g * (1.0 - u)
+    du = g * (h.astype(F32) - n)
+    dnpre = dn * (1.0 - n * n)
+    dupre = du * u * (1.0 - u)
+    drpre = dnpre * ghn * r * (1.0 - r)
+    dgi = jnp.concatenate([drpre, dupre, dnpre], axis=1).astype(BF)
+    dgh = jnp.concatenate([drpre, dupre, dnpre * r], axis=1).astype(BF)
+    dm = dot(dgi, wi, 1, 1).astype(BF)
+    dh = g * u + dot(dgh, wh, 1, 1)
+    return dgi, dgh, dm, dh
+
+
+def local_kernel(
+    x_ref, f_ref, src_ref, tgt_ref, val_ref, lab_ref, w1_ref, b1_ref, w2_hbm, b2_ref,
+    wi_ref, bi_ref, wh_ref, bh_ref, cot_ref,
+    fi_out, h1_out, dt2_out, dt1_out, h2_out, d1_out, d0_out, sm_out, w1_out,
+    w2, amat, acc, zaug, zpre_s, hs, hsl, dms, dml, xbuf, dzacc, picks, puts, sem,
+):
+    s = lax.axis_index("section")
+    w2_copy = pltpu.make_async_copy(w2_hbm, w2, sem)
+    w2_copy.start()
+    edges = f_ref.shape[2]
+    nodes = x_ref.shape[1]
+    feats = f_ref[s]
+    ends = pack_ends(src_ref, tgt_ref, val_ref, lab_ref, s)
+    fi_out[0:16] = feats
+    fi_out[16:32] = ends.astype(BF)
+    pick, put = edge_tables(ends, nodes)
+    picks[...] = pick
+    puts[...] = put
+    zpre = edge_hidden(feats, w1_ref[...], b1_ref[...])
+    zpre_s[...] = zpre
+    zaug[0:LANE] = jax.nn.silu(zpre).astype(BF)
+    zaug[LANE : 2 * LANE] = jnp.ones((LANE, edges), BF)
+    h0 = x_ref[s]
+
+    def sources(t, h):
+        got = dot(h, picks[...], 0, 0)
+        hs[t] = got
+        hsl[:, t * edges : (t + 1) * edges] = got.astype(BF)
+
+    sources(0, h0)
+    lane = lax.broadcasted_iota(jnp.int32, (LANE, LANE), 1)
+    b2t = b2_ref[...].T
+    w2_copy.wait()
+    tiles = [(e, min(256, edges - e)) for e in range(0, edges, 256)]
+
+    def keep(i, e, w, p):
+        p = p.reshape(16, 8, w).sum(0)
+        for o in range(0, w, LANE):
+            acc[(e + o) // LANE, aligned(i, 8), :] = p[:, o : o + LANE]
+
+    def first(ib):
+        lhs = []
+        for v in range(ROUND):
+            i = ib * ROUND + v
+            bias = jnp.where(lane == i, b2t, jnp.zeros_like(b2t))
+            lhs.append(jnp.concatenate([w2[:, aligned(i, LANE)].T, bias], axis=1))
+        lhs = jnp.concatenate(lhs, axis=0)
+        for e, w in tiles:
+            a = dot(lhs, zaug[:, e : e + w]).astype(BF)
+            amat[aligned(ib, ROUND * LANE), e : e + w] = a
+            for v in range(ROUND):
+                p = a[v * LANE : (v + 1) * LANE].astype(F32) * hs[0, :, e : e + w]
+                keep(ib * ROUND + v, e, w, p)
+
+    loop(LANE // ROUND, first)
+
+    def again(ib):
+        for e, w in tiles:
+            for v in range(8):
+                a = amat[aligned(ib * 8 + v, LANE), e : e + w]
+                p = a.astype(F32) * hs[1, :, e : e + w]
+                keep(ib * 8 + v, e, w, p)
+
+    def gathered():
+        msg = []
+        for e in range(edges // LANE):
+            part = acc[e, pl.ds(0, LANE, stride=8), :]
+            for q in range(1, 8):
+                part = part + acc[e, pl.ds(q, LANE, stride=8), :]
+            msg.append(part)
+        msg = jnp.concatenate(msg, axis=1)
+        total = jnp.zeros((nodes, LANE), F32)
+        for piece in split(msg, 3):
+            total = total + dot(puts[...], piece, 1, 1)
+        return total.astype(BF)
+
+    weights = (wi_ref[...], bi_ref[...], wh_ref[...], bh_ref[...])
+    m1 = gathered()
+    gates1 = gru_forward(m1, h0, *weights)
+    h1 = gates1[0].astype(BF)
+    h1_out[...] = h1
+    sources(1, h1)
+    loop(LANE // 8, again)
+    m2 = gathered()
+    gates2 = gru_forward(m2, h1, *weights)
+    h2_out[...] = gates2[0]
+    label = jnp.broadcast_to(ends[2:3, :nodes], (LANE, nodes)).T
+    g2 = cot_ref[s] * label
+    dgi2, dgh2, dm2, dh2 = gru_backward(g2, h1, gates2, weights[0], weights[2])
+    dt2 = dm2.T
+    dt2_out[...] = dt2
+
+    def spread(t, dt):
+        got = dot(dt, puts[...])
+        dms[t] = got
+        dml[:, t * edges : (t + 1) * edges] = got.astype(BF)
+
+    def to_sources(t):
+        outs = []
+        for e in range(0, edges, LANE):
+
+            def body(ib, total):
+                d = dms[t, aligned(ib, 8), e : e + LANE]
+                for v in range(8):
+                    a = amat[aligned(ib * 8 + v, LANE), e : e + LANE].astype(F32)
+                    total = total + a * d[v : v + 1]
+                return total
+
+            outs.append(lax.fori_loop(0, LANE // 8, body, jnp.zeros((LANE, LANE), F32)))
+        back = jnp.concatenate(outs, axis=1)
+        total = jnp.zeros((nodes, LANE), F32)
+        for piece in split(back, 3):
+            total = total + dot(picks[...], piece, 1, 1)
+        return total
+
+    spread(1, dt2)
+    d1 = (dh2 + to_sources(1)).astype(BF)
+    d1_out[...] = d1.astype(F32)
+    dgi1, dgh1, dm1, dh1 = gru_backward(d1.astype(F32), h0, gates1, weights[0], weights[2])
+    dt1 = dm1.T
+    dt1_out[...] = dt1
+    spread(0, dt1)
+    d0_out[...] = dh1 + to_sources(0)
+
+    gwi = dot(m1, dgi1, 0, 0) + dot(m2, dgi2, 0, 0)
+    gwh = dot(h0, dgh1, 0, 0) + dot(h1, dgh2, 0, 0)
+    for q in range(3):
+        sm_out[q * LANE : (q + 1) * LANE] = gwi[:, q * LANE : (q + 1) * LANE]
+        sm_out[(3 + q) * LANE : (4 + q) * LANE] = gwh[:, q * LANE : (q + 1) * LANE]
+    sm_out[6 * LANE : 7 * LANE] = dot(dml[...], hsl[...], 1, 1)
+    gbi = dgi1.astype(F32).sum(0, keepdims=True) + dgi2.astype(F32).sum(0, keepdims=True)
+    gbh = dgh1.astype(F32).sum(0, keepdims=True) + dgh2.astype(F32).sum(0, keepdims=True)
+    rows = [x[:, q * LANE : (q + 1) * LANE] for x in (gbi, gbh) for q in range(3)]
+    rows.append(jnp.zeros((SMALL_ROWS - 7 * LANE - 6, LANE), F32))
+    sm_out[7 * LANE :] = jnp.concatenate(rows, axis=0)
+
+    dzacc[...] = jnp.zeros_like(dzacc)
+
+    def back_hidden(ib):
+        for t in range(2):
+            h = hsl[:, t * edges : (t + 1) * edges].astype(F32)
+            d = dms[t, aligned(ib, ROUND), :]
+            for v in range(ROUND):
+                xbuf[v * LANE : (v + 1) * LANE, t * edges : (t + 1) * edges] = (
+                    h * d[v : v + 1]
+                ).astype(BF)
+        dzacc[...] += dot(w2[:, aligned(ib, ROUND * LANE)], xbuf[...])
+
+    loop(LANE // ROUND, back_hidden)
+    zp = zpre_s[...]
+    sig = jax.nn.sigmoid(zp)
+    slope = sig * (1.0 + zp * (1.0 - sig))
+    lhs = jnp.concatenate(
+        [feats, jnp.ones((1, edges), BF), jnp.zeros((15, edges), BF)], axis=0
+    )
+    total = jnp.zeros((32, LANE), F32)
+    for t in range(2):
+        dzpre = (dzacc[:, t * edges : (t + 1) * edges] * slope).astype(BF)
+        total = total + dot(lhs, dzpre, 1, 1)
+    w1_out[...] = total
+
+
+def shard_kernel(fi_ref, h0_ref, h1_ref, dt1_ref, dt2_ref, w1_ref, b1_ref, out_ref, qst, tmp):
+    s, c = lax.axis_index("section"), lax.axis_index("dp")
+    blocks, _, edges = fi_ref.shape
+    nodes = h0_ref.shape[1]
+    per = LANE // blocks
+    first_k = (c * 2 + s) * per
+    rows = lax.broadcasted_iota(jnp.int32, (8, LANE), 0) + first_k
+    sel = (rows == lax.broadcasted_iota(jnp.int32, (8, LANE), 1)).astype(F32)
+    w1t = dot(sel.astype(BF), w1_ref[...], 1, 1).astype(BF)
+    b1 = jnp.sum(sel * b1_ref[...].astype(F32), axis=1, keepdims=True)
+    quarter = nodes // 4
+    qn = lax.broadcasted_iota(jnp.int32, (quarter, 256), 0).astype(F32)
+
+    def build(blk):
+        z = jax.nn.silu(dot(w1t, fi_ref[blk, 0:16]) + b1).astype(BF).astype(F32)
+        ends = fi_ref[blk, 16:32].astype(F32)
+        for q in range(4):
+            lo = q * LANE
+            zq = z[:, lo : lo + 256]
+            hit_t = (qn + float(q * quarter)) == ends[1:2, lo : lo + 256]
+            hit_s = (qn + float(q * quarter)) == ends[0:1, lo : lo + 256]
+            lhs = [jnp.where(hit_t, zq[k : k + 1], 0.0).astype(BF) for k in range(per)]
+            lhs = jnp.concatenate(lhs, axis=0)
+            pairs = dot(lhs, hit_s.astype(F32).astype(BF), 1, 1)
+            pairs = jnp.concatenate(split(pairs, 2), axis=1)
+            row = aligned(q, quarter)
+            h = jnp.concatenate([h0_ref[blk, row, :], h1_ref[blk, row, :]], axis=1)
+            got = dot(pairs, jnp.concatenate([h, h], axis=0)).astype(BF)
+            for t in range(2):
+                for k in range(per):
+                    qst[t, pl.ds(pl.multiple_of(blk * nodes + q * quarter, quarter), quarter), k * LANE : (k + 1) * LANE] = got[k * quarter : (k + 1) * quarter, t * LANE : (t + 1) * LANE]
+
+    loop(blocks, build)
+    total = jnp.zeros((LANE, per * LANE), F32)
+    for t, ref in ((0, dt1_ref), (1, dt2_ref)):
+        lhs = jnp.concatenate([ref[blk] for blk in range(blocks)], axis=1)
+        total = total + dot(lhs, qst[t])
+    count = jnp.zeros((1, 1), F32)
+    for blk in range(blocks):
+        count = count + jnp.sum(fi_ref[blk, 16:32].astype(F32)[2:3, :nodes], axis=1, keepdims=True)
+    total = total / count
+    for k in range(per):
+        tmp[pl.ds(k, LANE, stride=per), :] = total[:, k * LANE : (k + 1) * LANE]
+    out_ref[...] = tmp[...].astype(BF)
+
+
+def final_kernel(a_ref, b_ref, out_ref):
+    per = a_ref.shape[1] // LANE
+    a = a_ref[0].astype(F32)
+    b = b_ref[0].astype(F32)
+    for i in range(LANE):
+        out_ref[:, i * LANE : (i + 1) * LANE] = jnp.concatenate(
+            [a[i * per : (i + 1) * per], b[i * per : (i + 1) * per]], axis=0
+        )
+
+
+def shards(
+    node_input, edge_input, edge_source, edge_target, edge_valid, node_labeled,
+    edge_w1, edge_b1, edge_w2, edge_b2, gru_wi, gru_bi, gru_wh, gru_bh, state_cot,
+):
+    micro, nodes, width = node_input.shape
+    edges = edge_input.shape[2]
+    parts = lax.axis_size("dp")
+    blocks = 2 * parts
+    per = width // blocks
+    vm = pl.BlockSpec(memory_space=VMEM)
+    limit = pltpu.CompilerParams(vmem_limit_bytes=60 * 2**20)
+    sds = jax.ShapeDtypeStruct
+    b1 = edge_b1.reshape(1, -1)
+    fi, h1, dt2, dt1, h2, d1, d0, small, gw1 = pl.pallas_call(
+        local_kernel,
+        out_shape=(
+            sds((32, edges), BF), sds((nodes, width), BF), sds((width, nodes), BF),
+            sds((width, nodes), BF), sds((nodes, width), F32), sds((nodes, width), F32),
+            sds((nodes, width), F32), sds((SMALL_ROWS, width), F32), sds((32, width), F32),
+        ),
+        in_specs=[vm] * 8 + [pl.BlockSpec(memory_space=pl.ANY)] + [vm] * 6,
+        out_specs=[vm] * 9,
+        scratch_shapes=[
+            VMEM((width, width * width), BF), VMEM((width * width, edges), BF),
+            VMEM((edges // LANE, 8 * width, LANE), F32), VMEM((2 * width, edges), BF),
+            VMEM((width, edges), F32), VMEM((2, width, edges), F32),
+            VMEM((width, 2 * edges), BF), VMEM((2, width, edges), F32),
+            VMEM((width, 2 * edges), BF), VMEM((ROUND * width, 2 * edges), BF),
+            VMEM((width, 2 * edges), F32), VMEM((nodes, edges), BF), VMEM((nodes, edges), BF),
+            pltpu.SemaphoreType.DMA,
+        ],
+        compiler_params=limit,
+    )(
+        node_input, edge_input, edge_source, edge_target, edge_valid, node_labeled,
+        edge_w1, b1, edge_w2, edge_b2.reshape(width, width),
+        gru_wi, gru_bi.reshape(1, -1), gru_wh, gru_bh.reshape(1, -1), state_cot,
+    )
+    every = ("section", "dp")
+    fi_all = lax.all_gather(fi, every)
+    h1_all = lax.all_gather(h1, every)
+    dt2_all = lax.all_gather(dt2, every)
+    dt1_all = lax.all_gather(dt1, every)
+    h0_all = lax.all_gather(node_input, "dp", axis=1).reshape(blocks, nodes, width)
+    shard = pl.pallas_call(
+        shard_kernel,
+        out_shape=sds((width * per, width), BF),
+        in_specs=[vm] * 7,
+        out_specs=vm,
+        scratch_shapes=[
+            VMEM((2, blocks * nodes, per * width), BF), VMEM((width * per, width), F32)
+        ],
+        compiler_params=limit,
+    )(fi_all, h0_all, h1_all, dt1_all, dt2_all, edge_w1, b1)
+    full = lax.all_gather(shard, every)
+    grad_w2 = pl.pallas_call(
+        final_kernel,
+        grid=(parts,),
+        out_shape=sds((width, width * width), F32),
+        in_specs=[
+            pl.BlockSpec((1, width * per, width), lambda c: (c, 0, 0)),
+            pl.BlockSpec((1, width * per, width), lambda c: (c + parts, 0, 0)),
+        ],
+        out_specs=pl.BlockSpec((2 * per, width * width), lambda c: (c, 0)),
+    )(full, full)
+    count = jnp.sum(fi_all[:, 18, :nodes].astype(F32))
+    small, gw1 = lax.psum((small, gw1), every)
+    small, gw1 = small / count, gw1 / count
+    h1f = h1.astype(F32)
+    mine = jnp.where(lax.axis_index("section") == 0, h1f, h2)
+    other = jnp.where(lax.axis_index("section") == 0, h2, h1f)
+    minex = jnp.where(lax.axis_index("section") == 0, d0, d1)
+    otherx = jnp.where(lax.axis_index("section") == 0, d1, d0)
+    got, gotx = lax.ppermute((other, otherx), "section", [(0, 1), (1, 0)])
+
+    def order(a, b):
+        return jnp.where(lax.axis_index("section") == 0, jnp.stack([a, b]), jnp.stack([b, a]))
+
+    def third(rows):
+        return rows.reshape(3, width, width).transpose(1, 0, 2).reshape(width, 3 * width)
+
+    return (
+        order(mine, got)[None],
+        order(minex, gotx)[None],
+        gw1[:16],
+        gw1[16],
+        grad_w2,
+        small[6 * width : 7 * width].reshape(-1),
+        third(small[: 3 * width]),
+        small[7 * width : 7 * width + 3].reshape(-1),
+        third(small[3 * width : 6 * width]),
+        small[7 * width + 3 : 7 * width + 6].reshape(-1),
+    )
+
 
 EDGE_BLOCK = 128
 
@@ -125,7 +521,7 @@
     return (d_total, (ends[1], ends[2], ends[3], ends[4], grad_wi, grad_bi, grad_wh, grad_bh))
 
 
-def shards(
+def plain_shards(
     node_input,
     edge_input,
     edge_source,
@@ -221,37 +617,14 @@
 
 def solution(mesh):
     placed = (
-        P(None, "dp", None),
-        P(None, None, "dp"),
-        P(None, "dp"),
-        P(None, "dp"),
-        P(None, "dp"),
-        P(None, "dp"),
-        P(),
-        P(),
-        P(),
-        P(),
-        P(),
-        P(),
-        P(),
-        P(),
-        P(None, "dp", None),
-    )
+        P(None, "dp", None), P(None, None, "dp"), P(None, "dp"), P(None, "dp"), P(None, "dp"),
+        P(None, "dp"), P(), P(), P(), P(), P(), P(), P(), P(), P(None, "dp", None),
+    )
+    fits = LANE % (2 * mesh.shape["dp"]) == 0
     return jax.shard_map(
-        shards,
+        shards if fits else plain_shards,
         mesh=mesh,
         in_specs=placed,
-        out_specs=(
-            P("section", None, "dp", None),
-            P("section", None, "dp", None),
-            P(),
-            P(),
-            P(),
-            P(),
-            P(),
-            P(),
-            P(),
-            P(),
-        ),
+        out_specs=(P("section", None, "dp", None), P("section", None, "dp", None)) + (P(),) * 8,
         check_vma=False,
     )

time: 953 us -> 509 us (0.53); the launches traced: 941 us -> 509 us
  matrix products: 449 us -> 0 us
  waiting for transfers between devices: 103 us -> 369 us
  other arithmetic: 193 us -> 5.21 us
  Pallas kernels: 0 us -> 73.1 us
  local copies, waits for them, and re-layouts: 78 us -> 6.76 us
  blocking collectives: 82.8 us -> 39.2 us
  loops' own time: 11.8 us -> 0 us
    dot_general x183 -> x0, matrix products: 449 us -> none  [the longest x15 165 us: back_block(): jnp.dot(z_low.T, d_amat, preferred_element_type=jnp.float32)]
    all_gather x0 -> x6, waiting for transfers between devices: none -> 300 us  [the longest x1 59.1 us: shards(): full = lax.all_gather(shard, every)]
    pallas_call x0 -> x3, Pallas kernels: none -> 73.1 us  [the longest x1 39 us: shards(): pl.pallas_call(local_kernel, out_shape=(sds((32, edges), BF), sds((nodes,...]
    reduce_sum x19 -> x1, other arithmetic: 74 us -> 1.48 us  [shards(): count = jnp.sum(fi_all[:, 18, :nodes].astype(F32))]
    while x93 -> x0, local copies, waits for them, and re-layouts: 70 us -> none
    convert_element_type x80 -> x0, other arithmetic: 45.8 us -> none  [the longest x30 23.2 us: block_front(): weights[3].astype(jnp.float32)]
    psum x2 -> x1, blocking collectives: 82.8 us -> 39.2 us  [shards(): small, gw1 = lax.psum((small, gw1), every)]
    scatter-add x30 -> x0, other arithmetic: 40.1 us -> none  [the longest x15 20.8 us: add(): jax.ops.segment_sum(message, target_b, num_segments=nodes)]
  transfers between devices with their start and end apart: 5 -> 9, of which waited for: 4 -> 7; matrix products, arithmetic and copies ran while one was open for 1% -> 2% of each run, Pallas kernels for 0% -> 12%
where the time goes in v1:
time: 509 us
  waiting for transfers between devices  369 us (72%)
  Pallas kernels  73.1 us (14%)
  blocking collectives  39.2 us (8%)
  between operations  14.2 us (3%)
  local copies, waits for them, and re-layouts  6.76 us (1%)
  other arithmetic  5.21 us (1%)
    psum x1, waiting for transfers between devices, shards(): small, gw1 = lax.psum((small, gw1), every)  65.8 us
    all_gather x1, waiting for transfers between devices, shards(): full = lax.all_gather(shard, every)  59.1 us
    all_gather x1, waiting for transfers between devices, shards(): fi_all = lax.all_gather(fi, every)  56.5 us
    all_gather x1, waiting for transfers between devices, shards(): h1_all = lax.all_gather(h1, every)  56.2 us
    all_gather x1, waiting for transfers between devices, shards(): dt1_all = lax.all_gather(dt1, every)  55.9 us
    all_gather x1, waiting for transfers between devices, shards(): dt2_all = lax.all_gather(dt2, every)  55.8 us
    psum x1, blocking collectives, shards(): small, gw1 = lax.psum((small, gw1), every)  39.2 us
    pallas_call x1, Pallas kernels, shards(): pl.pallas_call(local_kernel, out_shape=(sds((32, edges), BF), sds((nodes,...  39 us
  transfers between devices with their start and end apart: 9, of which 7 were waited for; matrix products, arithmetic and copies ran while one was open for 2% of the time, Pallas kernels for 12%

profile of v1, /device:TPU:0, one launch (start us, length us, event | category | flops | bytes accessed | tf_op | source)
XLA Modules:
  0.0 508.6 jit_solution(17692811185813411362)
XLA Ops:
  7.2 0.0 all-gather.15.cloned.1.call-start
  7.2 0.7 all-gather.15.cloned.1.call-update
  7.9 0.0 all-gather.19.cloned.1.call-start
  8.0 1.2 reshape.177.bi_ref
  9.2 1.2 reshape.178.bh_ref
  10.4 39.0 %shard_map.222 = (bf16[32,640]{1,0:T(8,128)(2,1)}, bf16[128,128]{1,0:T(8,128)(2,1)}, bf16[128,128]{1,0:T(8,128)(2,1)}, bf16[128,128]{1,0:T(8,128)(2,1)}, f32[128...) custom-call(bf16[2,128,128]{2,1,0:T(8,128)(2,1)} %x_ref.1, ...), custom_call_target="tpu_custom_call" | custom-call | tf_op jit(solution)/shard_map/pallas_call | solution.py:321
  49.4 0.0 copy-start
  49.4 0.0 copy-start.1
  49.4 0.0 copy-start.2
  49.5 0.0 copy-start.3
  49.5 0.0 all-gather.19.cloned.1.call-update
  49.5 0.0 all-gather.21.cloned.1.call-start
  49.5 0.7 all-gather.21.cloned.1.call-update
  50.2 0.0 all-gather.17.cloned.1.call-start
  50.3 0.5 all-gather.17.cloned.1.call-update
  50.8 0.0 all-gather.13.cloned.1.call-start
  50.9 0.5 all-gather.13.cloned.1.call-update
  51.4 0.0 all-reduce.2.cloned.1.call-start
  51.4 0.5 all-reduce.2.cloned.1.call-update
  52.0 0.0 all-gather.23.cloned.1.call-start
  52.0 16.9 %all-gather.15.cloned.1.call-done = bf16[2,2048,128]{2,1,0:T(8,128)(2,1)} async-done(((bf16[2,128,128]{2,1,0:T(8,128)(2,1)}), bf16[2,2048,128]{2,1,0:T(8,128)(2,1)}) %all-gather.15.cloned.1.call-update) | async-done | bytes 1048592 | tf_op jit(solution)/shard_map/all_gather | solution.py:350
  68.9 55.9 %all-gather.19.cloned.1.call-done = bf16[4096,128]{1,0:T(8,128)(2,1)} async-done(((bf16[128,128]{1,0:T(8,128)(2,1)}), bf16[4096,128]{1,0:T(8,128)(2,1)}) %all-gather.19.cloned.1.call-update) | async-done | bytes 1048592 | tf_op jit(solution)/shard_map/all_gather | solution.py:349
  124.8 55.8 %all-gather.21.cloned.1.call-done = bf16[4096,128]{1,0:T(8,128)(2,1)} async-done(((bf16[128,128]{1,0:T(8,128)(2,1)}), bf16[4096,128]{1,0:T(8,128)(2,1)}) %all-gather.21.cloned.1.call-update) | async-done | bytes 1048592 | tf_op jit(solution)/shard_map/all_gather | solution.py:348
  180.6 56.2 %all-gather.17.cloned.1.call-done = bf16[4096,128]{1,0:T(8,128)(2,1)} async-done(((bf16[128,128]{1,0:T(8,128)(2,1)}), bf16[4096,128]{1,0:T(8,128)(2,1)}) %all-gather.17.cloned.1.call-update) | async-done | bytes 1048592 | tf_op jit(solution)/shard_map/all_gather | solution.py:347
  236.8 56.5 %all-gather.13.cloned.1.call-done = bf16[1024,640]{1,0:T(8,128)(2,1)} async-done(((bf16[32,640]{1,0:T(8,128)(2,1)}), bf16[1024,640]{1,0:T(8,128)(2,1)}) %all-gather.13.cloned.1.call-update) | async-done | bytes 1310736 | tf_op jit(solution)/shard_map/all_gather | solution.py:346
  293.4 22.9 %shard_map.223 = bf16[512,128]{1,0:T(8,128)(2,1)} custom-call(bf16[32,32,640]{2,1,0:T(8,128)(2,1)} %bitcast.32, bf16[32,128,128]{2,1,0:T(8,128)(2,1)} %bitcast.34, bf16[32,128,128]{2,1,0:T(8,128)(2,1)} %bitcast.37, bf16[32,128,128]{2,1,0:T(8,128)(2,1)} %bitcast.35, bf16[32,128,128]{2,1,0:T(8,128)(2,1)} %bitcast.36, bf16[16,128]{1,0:T(8,128)(2,1)} %w1_ref.3, ...), custom_call_target="tpu_custom_call" | custom-call | tf_op jit(solution)/shard_map/pallas_call | solution.py:351
  316.3 0.0 all-gather.23.cloned.1.call-update
  316.3 0.3 collective-permute-start
  316.7 0.3 collective-permute-start.1
  317.0 39.2 %psum.14 = f32[32,128]{1,0:T(8,128)S(1)} all-reduce(f32[32,128]{1,0:T(8,128)S(1)} %copy-done.4), channel_id=1, replica_groups=mesh['section'=2,'dp'=16] {'section','dp'}, use_global_device_ids=true, to_apply=%region_0.0 | all-reduce | flops 4096 | bytes 32768 | tf_op jit(solution)/shard_map/psum | solution.py:373
  356.1 0.0 collective-permute-done
  356.1 0.7 maximum_select_fusion
  356.8 0.0 collective-permute-done.1
  356.8 0.7 maximum_select_fusion.1
  357.5 1.5 fusion.1
  359.0 0.6 broadcast_divide_fusion.1
  359.6 0.6 slice.33
  360.2 65.8 %all-reduce.2.cloned.1.call-done = f32[1024,128]{1,0:T(8,128)} async-done(((f32[1024,128]{1,0:T(8,128)}), f32[1024,128]{1,0:T(8,128)}) %all-reduce.2.cloned.1.call-update) | async-done | bytes 524304 | tf_op jit(solution)/shard_map/psum | solution.py:373
  426.0 1.7 broadcast_divide_fusion
  427.8 0.1 copy.28
  427.9 0.8 copy.30
  428.8 0.1 copy.27
  428.9 0.8 copy.29
  429.7 0.5 slice_bitcast_fusion.3
  430.2 0.6 slice_bitcast_fusion.1
  430.8 0.6 slice_bitcast_fusion
  431.4 59.1 %all-gather.23.cloned.1.call-done = bf16[16384,128]{1,0:T(8,128)(2,1)} async-done(((bf16[512,128]{1,0:T(8,128)(2,1)}), bf16[16384,128]{1,0:T(8,128)(2,1)}) %all-gather.23.cloned.1.call-update) | async-done | bytes 4194320 | tf_op jit(solution)/shard_map/all_gather | solution.py:361
  490.6 11.2 %shard_map.224 = f32[128,16384]{1,0:T(8,128)} custom-call(bf16[32,512,128]{2,1,0:T(8,128)(2,1)} %bitcast.30, bf16[32,512,128]{2,1,0:T(8,128)(2,1)} %bitcast.31), custom_call_target="tpu_custom_call" | custom-call | tf_op jit(solution)/shard_map/pallas_call | solution.py:362
  (9 shorter events, 0.1 us)
Async XLA Ops:
  7.2 61.7 %all-gather.15.cloned.1.call-start = ((), (), s32[]{:S(2)}) async-start(), calls=%async_computation.2 | async-start | bytes 1114112 | tf_op jit(solution)/shard_map/all_gather | solution.py:350
  7.9 116.9 %all-gather.19.cloned.1.call-start = ((), (), s32[]{:S(2)}) async-start(), calls=%async_computation.4 | async-start | bytes 1081344 | tf_op jit(solution)/shard_map/all_gather | solution.py:349
  49.4 266.9 %copy-start = (bf16[128,128]{1,0:T(8,128)(2,1)S(1)}, bf16[128,128]{1,0:T(8,128)(2,1)}, u32[]{:S(2)}) copy-start(bf16[128,128]{1,0:T(8,128)(2,1)} %get-tuple-element.19) | copy-start | bytes 98308
  49.4 266.9 %copy-start.1 = (f32[128,128]{1,0:T(8,128)S(1)}, f32[128,128]{1,0:T(8,128)}, u32[]{:S(2)}) copy-start(f32[128,128]{1,0:T(8,128)} %get-tuple-element.20) | copy-start | bytes 196612
  49.4 267.2 %copy-start.2 = (f32[128,128]{1,0:T(8,128)S(1)}, f32[128,128]{1,0:T(8,128)}, u32[]{:S(2)}) copy-start(f32[128,128]{1,0:T(8,128)} %get-tuple-element.22) | copy-start | bytes 196612
  49.5 267.2 %copy-start.3 = (f32[128,128]{1,0:T(8,128)S(1)}, f32[128,128]{1,0:T(8,128)}, u32[]{:S(2)}) copy-start(f32[128,128]{1,0:T(8,128)} %get-tuple-element.21) | copy-start | bytes 196612
  49.5 267.5 %copy-start.4 = (f32[32,128]{1,0:T(8,128)S(1)}, f32[32,128]{1,0:T(8,128)}, u32[]{:S(2)}) copy-start(f32[32,128]{1,0:T(8,128)} %get-tuple-element.23) | copy-start | bytes 49156
  49.5 131.1 %all-gather.21.cloned.1.call-start = ((), (), s32[]{:S(2)}) async-start(), calls=%async_computation.5 | async-start | bytes 1081344 | tf_op jit(solution)/shard_map/all_gather | solution.py:348
  50.2 186.6 %all-gather.17.cloned.1.call-start = ((), (), s32[]{:S(2)}) async-start(), calls=%async_computation.3 | async-start | bytes 1081344 | tf_op jit(solution)/shard_map/all_gather | solution.py:347
  50.8 242.5 %all-gather.13.cloned.1.call-start = ((), (), s32[]{:S(2)}) async-start(), calls=%async_computation.1 | async-start | bytes 1351680 | tf_op jit(solution)/shard_map/all_gather | solution.py:346
  51.4 374.6 %all-reduce.2.cloned.1.call-start = ((), (), s32[]{:S(2)}) async-start(), calls=%async_computation | async-start | bytes 1048576 | tf_op jit(solution)/shard_map/psum | solution.py:373
  52.0 438.6 %all-gather.23.cloned.1.call-start = ((), (), s32[]{:S(2)}) async-start(), calls=%async_computation.6 | async-start | bytes 4325376 | tf_op jit(solution)/shard_map/all_gather | solution.py:361
  316.3 39.8 %collective-permute-start = (f32[128,128]{1,0:T(8,128)S(1)}, f32[128,128]{1,0:T(8,128)S(1)}, u32[]{:S(2)}, u32[]{:S(2)}) collective-permute-start(f32[128,128]{1,0:T(8,128)S(1)} %get-tuple-element.45), channel_id=1, source_target_pairs={{0,16},{16,0},{1,17},{17,1},{2,18},{18,2},{3,19},{19,3},{4,20},{20... | collective-permute-start | bytes 196616 | tf_op jit(solution)/shard_map/ppermute | solution.py:380
  316.7 40.1 %collective-permute-start.1 = (f32[128,128]{1,0:T(8,128)S(1)}, f32[128,128]{1,0:T(8,128)S(1)}, u32[]{:S(2)}, u32[]{:S(2)}) collective-permute-start(f32[128,128]{1,0:T(8,128)S(1)} %get-tuple-element.43), channel_id=1, source_target_pairs={{0,16},{16,0},{1,17},{17,1},{2,18},{18,2},{3,19},{19,3},{4,20},{20... | collective-permute-start | bytes 196616 | tf_op jit(solution)/shard_map/ppermute | solution.py:380
Sparse Core Ops, SparseCore 0:
  10.8 58.1 all-gather.14
  72.0 52.7 all-gather.18
  127.9 52.6 all-gather.20
  184.1 52.6 all-gather.16
  240.1 53.1 all-gather.12
  299.1 126.9 all-reduce.1
  429.5 61.0 all-gather.22

commit v2 on v1

--- a/solution.py
+++ b/solution.py
@@ -12,6 +12,8 @@
 LANE = 128
 ROUND = 16
 SMALL_ROWS = 1024
+PLANE = 4
+SEMS = 128
 
 
 def dot(a, b, ca=1, cb=0):
@@ -87,21 +89,149 @@
     return dgi, dgh, dm, dh
 
 
-def local_kernel(
+class Net:
+    def __init__(self, send_sems, recv_sems):
+        self.send_sems, self.recv_sems = send_sems, recv_sems
+        self.slots, self.sent = {}, []
+
+    def slot(self, key):
+        return self.slots.setdefault(key, len(self.slots))
+
+    def send(self, key, src, dst, peer):
+        copy = pltpu.make_async_remote_copy(
+            src_ref=src,
+            dst_ref=dst,
+            send_sem=self.send_sems.at[len(self.sent)],
+            recv_sem=self.recv_sems.at[self.slot(key)],
+            device_id=peer,
+            device_id_type=pl.DeviceIdType.MESH,
+        )
+        copy.start()
+        self.sent.append(copy)
+
+    def wait(self, key, region, peer):
+        pltpu.make_async_remote_copy(
+            src_ref=region,
+            dst_ref=region,
+            send_sem=self.send_sems.at[0],
+            recv_sem=self.recv_sems.at[self.slot(key)],
+            device_id=peer,
+            device_id_type=pl.DeviceIdType.MESH,
+        ).wait_recv()
+
+    def drain(self):
+        for copy in self.sent:
+            copy.wait_send()
+
+
+class Place:
+    def __init__(self, parts):
+        self.parts, self.plane = parts, PLANE
+        self.lines = parts // PLANE
+        self.s, self.c = lax.axis_index("section"), lax.axis_index("dp")
+        self.sibling = {"section": 1 - self.s}
+
+    def flip(self, mask):
+        at, bit = self.c, 1
+        while bit <= mask:
+            if mask & bit:
+                at = at + bit * (1 - 2 * lax.rem(lax.div(self.c, bit), 2))
+            bit *= 2
+        return at
+
+    def peer(self, mask):
+        return {"dp": self.flip(mask)}
+
+    def block(self, mask):
+        return self.s * self.parts + self.flip(mask)
+
+    def level(self, line):
+        own = lax.div(self.flip(line * self.plane), self.plane) * self.plane
+        return self.s * self.parts + own
+
+
+class Gather:
+    def __init__(self, net, place, name, buf):
+        self.net, self.place, self.name, self.buf = net, place, name, buf
+
+    def send(self, key, mask, peer):
+        ref = self.buf.at[self.place.block(mask)]
+        self.net.send((self.name,) + key, ref, ref, peer)
+
+    def recv(self, key, mask, peer):
+        self.net.wait((self.name,) + key, self.buf.at[self.place.block(mask)], peer)
+
+    def begin(self):
+        p = self.place
+        for line in range(1, p.lines):
+            self.send((line, 0), 0, p.peer(line * p.plane))
+        for q in range(1, p.plane):
+            self.send((0, q), 0, p.peer(q))
+
+    def along(self):
+        p = self.place
+        for line in range(1, p.lines):
+            mask = line * p.plane
+            self.recv((line, 0), mask, p.peer(mask))
+            for q in range(1, p.plane):
+                self.send((line, q), mask, p.peer(q))
+
+    def across(self):
+        p = self.place
+        for line in range(p.lines):
+            for q in range(1, p.plane):
+                self.recv((line, q), line * p.plane + q, p.peer(q))
+            ref = self.buf.at[pl.ds(p.level(line), p.plane)]
+            self.net.send((self.name, "sib", line), ref, ref, p.sibling)
+
+    def finish(self):
+        p = self.place
+        for line in range(p.lines):
+            first = p.level(line) + (1 - 2 * p.s) * p.parts
+            self.net.wait((self.name, "sib", line), self.buf.at[pl.ds(first, p.plane)], p.sibling)
+
+
+def main_kernel(
     x_ref, f_ref, src_ref, tgt_ref, val_ref, lab_ref, w1_ref, b1_ref, w2_hbm, b2_ref,
     wi_ref, bi_ref, wh_ref, bh_ref, cot_ref,
-    fi_out, h1_out, dt2_out, dt1_out, h2_out, d1_out, d0_out, sm_out, w1_out,
-    w2, amat, acc, zaug, zpre_s, hs, hsl, dms, dml, xbuf, dzacc, picks, puts, sem,
+    full_out, states_out, grads_out, w1_out,
+    w2, amat, acc, zaug, zpre_s, hs, hsl, dms, dml, xbuf, dzacc, picks, puts,
+    ins, hid, dts, qst, tmp, mine, small, small_in, small_lo, small_line, small_plane,
+    w1_io, swap, w2_sems, own_sem, send_sems, recv_sems,
 ):
-    s = lax.axis_index("section")
-    w2_copy = pltpu.make_async_copy(w2_hbm, w2, sem)
-    w2_copy.start()
-    edges = f_ref.shape[2]
-    nodes = x_ref.shape[1]
+    edges, nodes = f_ref.shape[2], x_ref.shape[1]
+    tiles5 = edges // LANE
+    parts = full_out.shape[0] // 2
+    blocks = 2 * parts
+    per = LANE // blocks
+    place = Place(parts)
+    net = Net(send_sems, recv_sems)
+    s, c = place.s, place.c
+    me = place.block(0)
+    rounds = LANE // ROUND
+
+    barrier = pltpu.get_barrier_semaphore()
+    peers = [place.peer(q) for q in range(1, PLANE)]
+    peers += [place.peer(line * PLANE) for line in range(1, place.lines)] + [place.sibling]
+    for peer in peers:
+        pl.semaphore_signal(
+            barrier, inc=1, device_id=peer, device_id_type=pl.DeviceIdType.MESH
+        )
+
+    def w2_copy(ib):
+        part = aligned(ib, ROUND * LANE)
+        return pltpu.make_async_copy(w2_hbm.at[:, part], w2.at[:, part], w2_sems.at[ib])
+
+    for ib in range(rounds):
+        w2_copy(ib).start()
+
     feats = f_ref[s]
     ends = pack_ends(src_ref, tgt_ref, val_ref, lab_ref, s)
-    fi_out[0:16] = feats
-    fi_out[16:32] = ends.astype(BF)
+    h0 = x_ref[s]
+    table = jnp.concatenate([feats, ends.astype(BF)], axis=0)
+    for e in range(tiles5):
+        ins[me, e * 32 : (e + 1) * 32, :] = table[:, e * LANE : (e + 1) * LANE]
+    ins[me, tiles5 * 32 : tiles5 * 32 + nodes, :] = h0
     pick, put = edge_tables(ends, nodes)
     picks[...] = pick
     puts[...] = put
@@ -109,7 +239,6 @@
     zpre_s[...] = zpre
     zaug[0:LANE] = jax.nn.silu(zpre).astype(BF)
     zaug[LANE : 2 * LANE] = jnp.ones((LANE, edges), BF)
-    h0 = x_ref[s]
 
     def sources(t, h):
         got = dot(h, picks[...], 0, 0)
@@ -119,8 +248,14 @@
     sources(0, h0)
     lane = lax.broadcasted_iota(jnp.int32, (LANE, LANE), 1)
     b2t = b2_ref[...].T
-    w2_copy.wait()
     tiles = [(e, min(256, edges - e)) for e in range(0, edges, 256)]
+
+    pl.semaphore_wait(barrier, len(peers))
+    gather_in = Gather(net, place, "in", ins)
+    gather_h1 = Gather(net, place, "h1", hid)
+    gather_d2 = Gather(net, place, "d2", dts.at[1])
+    gather_d1 = Gather(net, place, "d1", dts.at[0])
+    gather_in.begin()
 
     def keep(i, e, w, p):
         p = p.reshape(16, 8, w).sum(0)
@@ -128,6 +263,7 @@
             acc[(e + o) // LANE, aligned(i, 8), :] = p[:, o : o + LANE]
 
     def first(ib):
+        w2_copy(ib).wait()
         lhs = []
         for v in range(ROUND):
             i = ib * ROUND + v
@@ -141,18 +277,18 @@
                 p = a[v * LANE : (v + 1) * LANE].astype(F32) * hs[0, :, e : e + w]
                 keep(ib * ROUND + v, e, w, p)
 
-    loop(LANE // ROUND, first)
+    loop(rounds, first)
+    gather_in.along()
 
     def again(ib):
         for e, w in tiles:
             for v in range(8):
                 a = amat[aligned(ib * 8 + v, LANE), e : e + w]
-                p = a.astype(F32) * hs[1, :, e : e + w]
-                keep(ib * 8 + v, e, w, p)
+                keep(ib * 8 + v, e, w, a.astype(F32) * hs[1, :, e : e + w])
 
     def gathered():
         msg = []
-        for e in range(edges // LANE):
+        for e in range(tiles5):
             part = acc[e, pl.ds(0, LANE, stride=8), :]
             for q in range(1, 8):
                 part = part + acc[e, pl.ds(q, LANE, stride=8), :]
@@ -167,35 +303,38 @@
     m1 = gathered()
     gates1 = gru_forward(m1, h0, *weights)
     h1 = gates1[0].astype(BF)
-    h1_out[...] = h1
+    hid[me] = h1
+    gather_h1.begin()
     sources(1, h1)
     loop(LANE // 8, again)
+    gather_in.across()
+    gather_h1.along()
     m2 = gathered()
     gates2 = gru_forward(m2, h1, *weights)
-    h2_out[...] = gates2[0]
+    h2 = gates2[0]
     label = jnp.broadcast_to(ends[2:3, :nodes], (LANE, nodes)).T
     g2 = cot_ref[s] * label
     dgi2, dgh2, dm2, dh2 = gru_backward(g2, h1, gates2, weights[0], weights[2])
     dt2 = dm2.T
-    dt2_out[...] = dt2
+    dts[1, me] = dt2
+    gather_d2.begin()
 
     def spread(t, dt):
         got = dot(dt, puts[...])
         dms[t] = got
         dml[:, t * edges : (t + 1) * edges] = got.astype(BF)
 
-    def to_sources(t):
-        outs = []
-        for e in range(0, edges, LANE):
-
-            def body(ib, total):
-                d = dms[t, aligned(ib, 8), e : e + LANE]
-                for v in range(8):
-                    a = amat[aligned(ib * 8 + v, LANE), e : e + LANE].astype(F32)
-                    total = total + a * d[v : v + 1]
-                return total
-
-            outs.append(lax.fori_loop(0, LANE // 8, body, jnp.zeros((LANE, LANE), F32)))
+    def to_source_tile(t, e):
+        def body(ib, total):
+            d = dms[t, aligned(ib, 8), e * LANE : (e + 1) * LANE]
+            for v in range(8):
+                a = amat[aligned(ib * 8 + v, LANE), e * LANE : (e + 1) * LANE].astype(F32)
+                total = total + a * d[v : v + 1]
+            return total
+
+        return lax.fori_loop(0, LANE // 8, body, jnp.zeros((LANE, LANE), F32))
+
+    def to_nodes(outs):
         back = jnp.concatenate(outs, axis=1)
         total = jnp.zeros((nodes, LANE), F32)
         for piece in split(back, 3):
@@ -203,25 +342,160 @@
         return total
 
     spread(1, dt2)
-    d1 = (dh2 + to_sources(1)).astype(BF)
-    d1_out[...] = d1.astype(F32)
+    back2 = [to_source_tile(1, e) for e in range(tiles5)]
+    gather_d2.along()
+    gather_h1.across()
+    d1 = (dh2 + to_nodes(back2)).astype(BF)
     dgi1, dgh1, dm1, dh1 = gru_backward(d1.astype(F32), h0, gates1, weights[0], weights[2])
     dt1 = dm1.T
-    dt1_out[...] = dt1
-    spread(0, dt1)
-    d0_out[...] = dh1 + to_sources(0)
-
+    dts[0, me] = dt1
+    gather_d1.begin()
+
+    half = SMALL_ROWS // 2
+    plane_rows = half // place.lines
+    own_rows = plane_rows // PLANE
     gwi = dot(m1, dgi1, 0, 0) + dot(m2, dgi2, 0, 0)
     gwh = dot(h0, dgh1, 0, 0) + dot(h1, dgh2, 0, 0)
     for q in range(3):
-        sm_out[q * LANE : (q + 1) * LANE] = gwi[:, q * LANE : (q + 1) * LANE]
-        sm_out[(3 + q) * LANE : (4 + q) * LANE] = gwh[:, q * LANE : (q + 1) * LANE]
-    sm_out[6 * LANE : 7 * LANE] = dot(dml[...], hsl[...], 1, 1)
+        small[q * LANE : (q + 1) * LANE] = gwi[:, q * LANE : (q + 1) * LANE]
+        small[(3 + q) * LANE : (4 + q) * LANE] = gwh[:, q * LANE : (q + 1) * LANE]
+    spread(0, dt1)
+    small[6 * LANE : 7 * LANE] = dot(dml[...], hsl[...], 1, 1)
     gbi = dgi1.astype(F32).sum(0, keepdims=True) + dgi2.astype(F32).sum(0, keepdims=True)
     gbh = dgh1.astype(F32).sum(0, keepdims=True) + dgh2.astype(F32).sum(0, keepdims=True)
     rows = [x[:, q * LANE : (q + 1) * LANE] for x in (gbi, gbh) for q in range(3)]
     rows.append(jnp.zeros((SMALL_ROWS - 7 * LANE - 6, LANE), F32))
-    sm_out[7 * LANE :] = jnp.concatenate(rows, axis=0)
+    small[7 * LANE :] = jnp.concatenate(rows, axis=0)
+    net.send(("small", "sib"), small.at[aligned(1 - s, half)], small_in, place.sibling)
+
+    back1 = [to_source_tile(0, e) for e in range(3)]
+    gather_d1.along()
+    gather_d2.across()
+    net.wait(("small", "sib"), small_in, place.sibling)
+    small_lo[...] = (small[aligned(s, half), :] + small_in[...]).astype(BF)
+    z = lax.div(c, PLANE)
+    for line in range(1, place.lines):
+        to = lax.div(place.flip(line * PLANE), PLANE)
+        net.send(
+            ("small", "line", line),
+            small_lo.at[aligned(to, plane_rows)],
+            small_line.at[line],
+            place.peer(line * PLANE),
+        )
+    back1 += [to_source_tile(0, e) for e in range(3, tiles5)]
+    d0 = dh1 + to_nodes(back1)
+    gather_in.finish()
+    gather_h1.finish()
+
+    zero = s == 0
+    swap[0, 0] = jnp.where(zero, h2, h1.astype(F32))
+    swap[0, 1] = jnp.where(zero, d1.astype(F32), d0)
+    net.send(("swap",), swap.at[0], swap.at[1], place.sibling)
+
+    first_k = (c * 2 + s) * per
+    ks = lax.broadcasted_iota(jnp.int32, (8, LANE), 0) + first_k
+    sel = (ks == lax.broadcasted_iota(jnp.int32, (8, LANE), 1)).astype(F32)
+    w1t = dot(sel.astype(BF), w1_ref[...], 1, 1).astype(BF)
+    b1 = jnp.sum(sel * b1_ref[...].astype(F32), axis=1, keepdims=True)
+    quarter = nodes // 4
+    qn = lax.broadcasted_iota(jnp.int32, (quarter, 256), 0).astype(F32)
+    sn = lax.broadcasted_iota(jnp.int32, (nodes, 256), 0).astype(F32)
+
+    def build(blk):
+        cols = [ins[blk, e * 32 : (e + 1) * 32, :] for e in range(tiles5)]
+        fi = jnp.concatenate(cols, axis=1)
+        z = jax.nn.silu(dot(w1t, fi[0:16]) + b1).astype(BF).astype(F32)
+        en = fi[16:32].astype(F32)
+        pairs = []
+        for q in range(4):
+            lo = q * LANE
+            zq = z[:, lo : lo + 256]
+            hit_t = (qn + float(q * quarter)) == en[1:2, lo : lo + 256]
+            hit_s = (sn == en[0:1, lo : lo + 256]).astype(F32).astype(BF)
+            lhs = [jnp.where(hit_t, zq[k : k + 1], 0.0).astype(BF) for k in range(per)]
+            pairs.append(dot(jnp.concatenate(lhs, axis=0), hit_s, 1, 1))
+        pairs = jnp.concatenate(split(jnp.concatenate(pairs, axis=0), 2), axis=1)
+        h = jnp.concatenate([ins[blk, tiles5 * 32 : tiles5 * 32 + nodes, :], hid[blk]], axis=1)
+        got = dot(pairs, jnp.concatenate([h, h], axis=0)).astype(BF)
+        for q in range(4):
+            at = pl.ds(pl.multiple_of(blk * nodes + q * quarter, quarter), quarter)
+            for k in range(per):
+                part = got[(q * per + k) * quarter : (q * per + k + 1) * quarter]
+                for t in range(2):
+                    qst[t, at, k * LANE : (k + 1) * LANE] = part[:, t * LANE : (t + 1) * LANE]
+
+    loop(blocks, build)
+    gather_d1.across()
+    gather_d2.finish()
+    lhs = jnp.concatenate([dts[1, blk] for blk in range(blocks)], axis=1)
+    total = dot(lhs, qst[1])
+    count = jnp.zeros((1, LANE), F32)
+    for blk in range(blocks):
+        count = count + ins[blk, 16:32, :].astype(F32)[2:3]
+    scale = 1.0 / jnp.sum(count, axis=1, keepdims=True)
+
+    own = small_lo[aligned(z, plane_rows), :].astype(F32)
+    for line in range(1, place.lines):
+        net.wait(("small", "line", line), small_line.at[line], place.peer(line * PLANE))
+        own = own + small_line[line].astype(F32)
+    small_line[0] = own.astype(BF)
+    q_me = lax.rem(c, PLANE)
+    for q in range(1, PLANE):
+        to = lax.rem(place.flip(q), PLANE)
+        net.send(
+            ("small", "plane", q),
+            small_line.at[0, aligned(to, own_rows)],
+            small_plane.at[q],
+            place.peer(q),
+        )
+    gather_d1.finish()
+    lhs = jnp.concatenate([dts[0, blk] for blk in range(blocks)], axis=1)
+    total = (total + dot(lhs, qst[0])) * scale
+    for k in range(per):
+        tmp[pl.ds(k, LANE, stride=per), :] = total[:, k * LANE : (k + 1) * LANE]
+    mine[0 : per * LANE] = tmp[...].astype(BF)
+    own = small_line[0, aligned(q_me, own_rows), :].astype(F32)
+    for q in range(1, PLANE):
+        net.wait(("small", "plane", q), small_plane.at[q], place.peer(q))
+        own = own + small_plane[q].astype(F32)
+    mine[per * LANE : per * LANE + own_rows] = (own * scale).astype(BF)
+
+    size = mine.shape[0]
+    halves = (pl.ds(0, size // 2), pl.ds(size // 2, size // 2))
+    keep_own = pltpu.make_async_copy(mine, full_out.at[me], own_sem)
+    keep_own.start()
+    for line in range(1, place.lines):
+        net.send(("out", line), mine, full_out.at[me], place.peer(line * PLANE))
+    for q in (1, 2):
+        for a in range(2):
+            net.send(
+                ("out", 0, q, a), mine.at[halves[a]], full_out.at[me, halves[a]], place.peer(q)
+            )
+
+    def out_line(line):
+        mask = line * PLANE
+        blk = place.block(mask)
+        net.wait(("out", line), full_out.at[blk], place.peer(mask))
+        for q in (1, 2):
+            for a in range(2):
+                ref = full_out.at[blk, halves[a]]
+                net.send(("out", line, q, a), ref, ref, place.peer(q))
+
+    def out_cross(line):
+        for q, a in ((1, 0), (2, 1)):
+            ref = full_out.at[place.block(line * PLANE + q), halves[a]]
+            net.wait(("out", line, q, a), ref, place.peer(q))
+            net.send(("out", line, 3, a), ref, ref, place.peer(3 - q))
+
+    def out_level(line):
+        for q, a in ((1, 1), (2, 0)):
+            ref = full_out.at[place.block(line * PLANE + q), halves[a]]
+            net.wait(("out", line, q, a), ref, place.peer(q))
+        for q, a in ((2, 0), (1, 1)):
+            ref = full_out.at[place.block(line * PLANE + 3), halves[a]]
+            net.wait(("out", line, 3, a), ref, place.peer(q))
+        ref = full_out.at[pl.ds(place.level(line), PLANE)]
+        net.send(("out", "sib", line), ref, ref, place.sibling)
 
     dzacc[...] = jnp.zeros_like(dzacc)
 
@@ -235,7 +509,15 @@
                 ).astype(BF)
         dzacc[...] += dot(w2[:, aligned(ib, ROUND * LANE)], xbuf[...])
 
-    loop(LANE // ROUND, back_hidden)
+    loop(rounds // 4, back_hidden)
+    for line in range(1, place.lines):
+        out_line(line)
+    loop(rounds // 2, lambda ib: back_hidden(ib + rounds // 4))
+    keep_own.wait()
+    for line in range(place.lines):
+        out_cross(line)
+    loop(rounds // 4, lambda ib: back_hidden(ib + 3 * rounds // 4))
+
     zp = zpre_s[...]
     sig = jax.nn.sigmoid(zp)
     slope = sig * (1.0 + zp * (1.0 - sig))
@@ -246,63 +528,68 @@
     for t in range(2):
         dzpre = (dzacc[:, t * edges : (t + 1) * edges] * slope).astype(BF)
         total = total + dot(lhs, dzpre, 1, 1)
-    w1_out[...] = total
-
-
-def shard_kernel(fi_ref, h0_ref, h1_ref, dt1_ref, dt2_ref, w1_ref, b1_ref, out_ref, qst, tmp):
-    s, c = lax.axis_index("section"), lax.axis_index("dp")
-    blocks, _, edges = fi_ref.shape
-    nodes = h0_ref.shape[1]
-    per = LANE // blocks
-    first_k = (c * 2 + s) * per
-    rows = lax.broadcasted_iota(jnp.int32, (8, LANE), 0) + first_k
-    sel = (rows == lax.broadcasted_iota(jnp.int32, (8, LANE), 1)).astype(F32)
-    w1t = dot(sel.astype(BF), w1_ref[...], 1, 1).astype(BF)
-    b1 = jnp.sum(sel * b1_ref[...].astype(F32), axis=1, keepdims=True)
-    quarter = nodes // 4
-    qn = lax.broadcasted_iota(jnp.int32, (quarter, 256), 0).astype(F32)
-
-    def build(blk):
-        z = jax.nn.silu(dot(w1t, fi_ref[blk, 0:16]) + b1).astype(BF).astype(F32)
-        ends = fi_ref[blk, 16:32].astype(F32)
-        for q in range(4):
-            lo = q * LANE
-            zq = z[:, lo : lo + 256]
-            hit_t = (qn + float(q * quarter)) == ends[1:2, lo : lo + 256]
-            hit_s = (qn + float(q * quarter)) == ends[0:1, lo : lo + 256]
-            lhs = [jnp.where(hit_t, zq[k : k + 1], 0.0).astype(BF) for k in range(per)]
-            lhs = jnp.concatenate(lhs, axis=0)
-            pairs = dot(lhs, hit_s.astype(F32).astype(BF), 1, 1)
-            pairs = jnp.concatenate(split(pairs, 2), axis=1)
-            row = aligned(q, quarter)
-            h = jnp.concatenate([h0_ref[blk, row, :], h1_ref[blk, row, :]], axis=1)
-            got = dot(pairs, jnp.concatenate([h, h], axis=0)).astype(BF)
-            for t in range(2):
-                for k in range(per):
-                    qst[t, pl.ds(pl.multiple_of(blk * nodes + q * quarter, quarter), quarter), k * LANE : (k + 1) * LANE] = got[k * quarter : (k + 1) * quarter, t * LANE : (t + 1) * LANE]
-
-    loop(blocks, build)
-    total = jnp.zeros((LANE, per * LANE), F32)
-    for t, ref in ((0, dt1_ref), (1, dt2_ref)):
-        lhs = jnp.concatenate([ref[blk] for blk in range(blocks)], axis=1)
-        total = total + dot(lhs, qst[t])
-    count = jnp.zeros((1, 1), F32)
-    for blk in range(blocks):
-        count = count + jnp.sum(fi_ref[blk, 16:32].astype(F32)[2:3, :nodes], axis=1, keepdims=True)
-    total = total / count
-    for k in range(per):
-        tmp[pl.ds(k, LANE, stride=per), :] = total[:, k * LANE : (k + 1) * LANE]
-    out_ref[...] = tmp[...].astype(BF)
-
-
-def final_kernel(a_ref, b_ref, out_ref):
-    per = a_ref.shape[1] // LANE
-    a = a_ref[0].astype(F32)
-    b = b_ref[0].astype(F32)
-    for i in range(LANE):
-        out_ref[:, i * LANE : (i + 1) * LANE] = jnp.concatenate(
-            [a[i * per : (i + 1) * per], b[i * per : (i + 1) * per]], axis=0
-        )
+    w1_io[0] = total[0:24]
+    net.send(("w1", "sib"), w1_io.at[0], w1_io.at[1], place.sibling)
+    net.wait(("w1", "sib"), w1_io.at[1], place.sibling)
+    total = w1_io[0] + w1_io[1]
+    w1_io[2] = total
+    at = 4
+    for line in range(1, place.lines):
+        net.send(("w1", "line", line), w1_io.at[2], w1_io.at[at + line], place.peer(line * PLANE))
+    for line in range(1, place.lines):
+        net.wait(("w1", "line", line), w1_io.at[at + line], place.peer(line * PLANE))
+        total = total + w1_io[at + line]
+    w1_io[3] = total
+    at += place.lines
+    for q in range(1, PLANE):
+        net.send(("w1", "plane", q), w1_io.at[3], w1_io.at[at + q], place.peer(q))
+    for q in range(1, PLANE):
+        net.wait(("w1", "plane", q), w1_io.at[at + q], place.peer(q))
+        total = total + w1_io[at + q]
+    w1_out[...] = total * scale
+
+    net.wait(("swap",), swap.at[1], place.sibling)
+    mine_state = jnp.where(zero, h1.astype(F32), h2)
+    mine_grad = jnp.where(zero, d0, d1.astype(F32))
+    states_out[0] = jnp.where(zero, mine_state, swap[1, 0])
+    states_out[1] = jnp.where(zero, swap[1, 0], mine_state)
+    grads_out[0] = jnp.where(zero, mine_grad, swap[1, 1])
+    grads_out[1] = jnp.where(zero, swap[1, 1], mine_grad)
+    for line in range(place.lines):
+        out_level(line)
+    for line in range(place.lines):
+        first = place.level(line) + (1 - 2 * s) * parts
+        net.wait(("out", "sib", line), full_out.at[pl.ds(first, PLANE)], place.sibling)
+    net.drain()
+
+
+def final_kernel(a_ref, b_ref, sm_ref, w1_ref, st_ref, sg_ref, w2_out, b2_out, wi_out, bi_out,
+                 wh_out, bh_out, gw1_out, gb1_out, st_out, sg_out):
+    low = lax.broadcasted_iota(jnp.int32, (1, 8, LANE), 1) < 4
+    rows = b2_out.shape[0] * 4
+    a = a_ref[0, :rows].astype(F32).reshape(rows // 8, 8, LANE)
+    b = b_ref[0, :rows].astype(F32).reshape(rows // 8, 8, LANE)
+    even = jnp.where(low, a, pltpu.roll(b, 4, 1))
+    odd = jnp.where(low, pltpu.roll(a, 4, 1), b)
+    for p in range(rows // 8):
+        w2_out[:, (2 * p) * LANE : (2 * p + 1) * LANE] = even[p]
+        w2_out[:, (2 * p + 1) * LANE : (2 * p + 2) * LANE] = odd[p]
+
+    @pl.when(pl.program_id(0) == 0)
+    def _():
+        own = sm_ref.shape[1]
+        x = sm_ref[...].astype(F32).reshape(-1, LANE)
+        for q in range(3):
+            cols = slice(q * LANE, (q + 1) * LANE)
+            wi_out[:, cols] = x[q * LANE : (q + 1) * LANE]
+            wh_out[:, cols] = x[(3 + q) * LANE : (4 + q) * LANE]
+            bi_out[:, cols] = x[7 * LANE + q : 7 * LANE + q + 1]
+            bh_out[:, cols] = x[7 * LANE + 3 + q : 7 * LANE + 4 + q]
+        b2_out[...] = x[6 * LANE : 7 * LANE]
+        gw1_out[...] = w1_ref[0:16]
+        gb1_out[...] = w1_ref[16:17]
+        st_out[...] = st_ref[...]
+        sg_out[...] = sg_ref[...]
 
 
 def shards(
@@ -314,19 +601,22 @@
     parts = lax.axis_size("dp")
     blocks = 2 * parts
     per = width // blocks
+    lines = parts // PLANE
+    half = SMALL_ROWS // 2
+    plane_rows = half // lines
+    own_rows = plane_rows // PLANE
+    size = width * per + own_rows
     vm = pl.BlockSpec(memory_space=VMEM)
-    limit = pltpu.CompilerParams(vmem_limit_bytes=60 * 2**20)
+    hbm = pl.BlockSpec(memory_space=pl.ANY)
     sds = jax.ShapeDtypeStruct
-    b1 = edge_b1.reshape(1, -1)
-    fi, h1, dt2, dt1, h2, d1, d0, small, gw1 = pl.pallas_call(
-        local_kernel,
+    full, states, grads, gw1 = pl.pallas_call(
+        main_kernel,
         out_shape=(
-            sds((32, edges), BF), sds((nodes, width), BF), sds((width, nodes), BF),
-            sds((width, nodes), BF), sds((nodes, width), F32), sds((nodes, width), F32),
-            sds((nodes, width), F32), sds((SMALL_ROWS, width), F32), sds((32, width), F32),
+            sds((blocks, size, width), BF), sds((2, nodes, width), F32),
+            sds((2, nodes, width), F32), sds((24, width), F32),
         ),
-        in_specs=[vm] * 8 + [pl.BlockSpec(memory_space=pl.ANY)] + [vm] * 6,
-        out_specs=[vm] * 9,
+        in_specs=[vm] * 8 + [hbm] + [vm] * 6,
+        out_specs=[hbm, vm, vm, vm],
         scratch_shapes=[
             VMEM((width, width * width), BF), VMEM((width * width, edges), BF),
             VMEM((edges // LANE, 8 * width, LANE), F32), VMEM((2 * width, edges), BF),
@@ -334,68 +624,55 @@
             VMEM((width, 2 * edges), BF), VMEM((2, width, edges), F32),
             VMEM((width, 2 * edges), BF), VMEM((ROUND * width, 2 * edges), BF),
             VMEM((width, 2 * edges), F32), VMEM((nodes, edges), BF), VMEM((nodes, edges), BF),
-            pltpu.SemaphoreType.DMA,
+            VMEM((blocks, 32 * (edges // LANE) + nodes, LANE), BF),
+            VMEM((blocks, nodes, width), BF), VMEM((2, blocks, width, nodes), BF),
+            VMEM((2, blocks * nodes, per * width), BF), VMEM((width * per, width), F32),
+            VMEM((size, width), BF), VMEM((SMALL_ROWS, width), F32), VMEM((half, width), F32),
+            VMEM((half, width), BF), VMEM((lines, plane_rows, width), BF),
+            VMEM((PLANE, own_rows, width), BF), VMEM((4 + lines + PLANE, 24, width), F32),
+            VMEM((2, 2, nodes, width), F32),
+            pltpu.SemaphoreType.DMA((width // ROUND,)), pltpu.SemaphoreType.DMA,
+            pltpu.SemaphoreType.DMA((SEMS,)), pltpu.SemaphoreType.DMA((SEMS,)),
         ],
-        compiler_params=limit,
+        compiler_params=pltpu.CompilerParams(
+            collective_id=0, has_side_effects=True, vmem_limit_bytes=62 * 2**20
+        ),
     )(
         node_input, edge_input, edge_source, edge_target, edge_valid, node_labeled,
-        edge_w1, b1, edge_w2, edge_b2.reshape(width, width),
+        edge_w1, edge_b1.reshape(1, -1), edge_w2, edge_b2.reshape(width, width),
         gru_wi, gru_bi.reshape(1, -1), gru_wh, gru_bh.reshape(1, -1), state_cot,
     )
-    every = ("section", "dp")
-    fi_all = lax.all_gather(fi, every)
-    h1_all = lax.all_gather(h1, every)
-    dt2_all = lax.all_gather(dt2, every)
-    dt1_all = lax.all_gather(dt1, every)
-    h0_all = lax.all_gather(node_input, "dp", axis=1).reshape(blocks, nodes, width)
-    shard = pl.pallas_call(
-        shard_kernel,
-        out_shape=sds((width * per, width), BF),
-        in_specs=[vm] * 7,
-        out_specs=vm,
-        scratch_shapes=[
-            VMEM((2, blocks * nodes, per * width), BF), VMEM((width * per, width), F32)
-        ],
-        compiler_params=limit,
-    )(fi_all, h0_all, h1_all, dt1_all, dt2_all, edge_w1, b1)
-    full = lax.all_gather(shard, every)
-    grad_w2 = pl.pallas_call(
+
+    def whole(*shape):
+        return pl.BlockSpec(shape, lambda c: (0,) * len(shape))
+
+    small = full[:, width * per :, :]
+    w2, b2, wi, bi, wh, bh, w1, b1, states, grads = pl.pallas_call(
         final_kernel,
         grid=(parts,),
-        out_shape=sds((width, width * width), F32),
+        out_shape=(
+            sds((width, width * width), F32), sds((width, width), F32),
+            sds((width, 3 * width), F32), sds((1, 3 * width), F32),
+            sds((width, 3 * width), F32), sds((1, 3 * width), F32),
+            sds((16, width), F32), sds((1, width), F32),
+            sds((2, nodes, width), F32), sds((2, nodes, width), F32),
+        ),
         in_specs=[
-            pl.BlockSpec((1, width * per, width), lambda c: (c, 0, 0)),
-            pl.BlockSpec((1, width * per, width), lambda c: (c + parts, 0, 0)),
+            pl.BlockSpec((1, size, width), lambda c: (c, 0, 0)),
+            pl.BlockSpec((1, size, width), lambda c: (c + parts, 0, 0)),
+            whole(blocks, own_rows, width), whole(24, width),
+            whole(2, nodes, width), whole(2, nodes, width),
         ],
-        out_specs=pl.BlockSpec((2 * per, width * width), lambda c: (c, 0)),
-    )(full, full)
-    count = jnp.sum(fi_all[:, 18, :nodes].astype(F32))
-    small, gw1 = lax.psum((small, gw1), every)
-    small, gw1 = small / count, gw1 / count
-    h1f = h1.astype(F32)
-    mine = jnp.where(lax.axis_index("section") == 0, h1f, h2)
-    other = jnp.where(lax.axis_index("section") == 0, h2, h1f)
-    minex = jnp.where(lax.axis_index("section") == 0, d0, d1)
-    otherx = jnp.where(lax.axis_index("section") == 0, d1, d0)
-    got, gotx = lax.ppermute((other, otherx), "section", [(0, 1), (1, 0)])
-
-    def order(a, b):
-        return jnp.where(lax.axis_index("section") == 0, jnp.stack([a, b]), jnp.stack([b, a]))
-
-    def third(rows):
-        return rows.reshape(3, width, width).transpose(1, 0, 2).reshape(width, 3 * width)
-
+        out_specs=(
+            pl.BlockSpec((2 * per, width * width), lambda c: (c, 0)), whole(width, width),
+            whole(width, 3 * width), whole(1, 3 * width), whole(width, 3 * width),
+            whole(1, 3 * width), whole(16, width), whole(1, width),
+            whole(2, nodes, width), whole(2, nodes, width),
+        ),
+    )(full, full, small, gw1, states, grads)
     return (
-        order(mine, got)[None],
-        order(minex, gotx)[None],
-        gw1[:16],
-        gw1[16],
-        grad_w2,
-        small[6 * width : 7 * width].reshape(-1),
-        third(small[: 3 * width]),
-        small[7 * width : 7 * width + 3].reshape(-1),
-        third(small[3 * width : 6 * width]),
-        small[7 * width + 3 : 7 * width + 6].reshape(-1),
+        states[None], grads[None], w1, b1.reshape(-1), w2, b2.reshape(-1),
+        wi, bi.reshape(-1), wh, bh.reshape(-1),
     )
 
 

time: 509 us -> 118 us (0.23)
  waiting for transfers between devices: 369 us -> 0 us
  blocking collectives: 39.2 us -> 0 us
  Pallas kernels: 73.1 us -> 110 us
  between operations: 14.2 us -> 0.66 us
    all_gather x6 -> x0, waiting for transfers between devices: 300 us -> none  [the longest x1 59.1 us: shards(): full = lax.all_gather(shard, every)]
    psum x1 -> x0, waiting for transfers between devices: 65.8 us -> none  [shards(): small, gw1 = lax.psum((small, gw1), every)]
    psum x1 -> x0, blocking collectives: 39.2 us -> none  [shards(): small, gw1 = lax.psum((small, gw1), every)]
    pallas_call x3 -> x2, Pallas kernels: 73.1 us -> 110 us  [the longest x1 98.1 us: shards(): pl.pallas_call(main_kernel, out_shape=(sds((blocks, size, width), BF), sd...]
  transfers between devices with their start and end apart: 9 -> 0, of which waited for: 7 -> 0; matrix products, arithmetic and copies ran while one was open for 2% -> 0% of each run, Pallas kernels for 12% -> 0%
where the time goes in v2:
time: 118 us; the launch traced here: 117 us
  Pallas kernels  110 us (93%)
  local copies, waits for them, and re-layouts  4.16 us (4%)
  other arithmetic  2.53 us (2%)
    pallas_call x1, Pallas kernels, shards(): pl.pallas_call(main_kernel, out_shape=(sds((blocks, size, width), BF), sd...  98.1 us
    pallas_call x1, Pallas kernels, shards(): pl.pallas_call(final_kernel, grid=(parts,), out_shape=(sds((width, width...  11.9 us
    pallas_call x2, other arithmetic, shards(): pl.pallas_call(final_kernel, grid=(parts,), out_shape=(sds((width, width...  2.53 us

profile of v2, /device:TPU:0, one launch (start us, length us, event | category | flops | bytes accessed | tf_op | source)
XLA Modules:
  0.0 117.4 jit_solution(1536978393139882848)
XLA Ops:
  0.6 1.2 %reshape.46.bi_ref = bf16[1,384]{1,0:T(2,128)(2,1)} reshape(bf16[384]{0:T(512)(128)(2,1)} %param.26) | data formatting | bytes 1536 | tf_op jit(solution)/shard_map/reshape | solution.py:643
  1.9 1.2 %reshape.47.bh_ref = bf16[1,384]{1,0:T(2,128)(2,1)} reshape(bf16[384]{0:T(512)(128)(2,1)} %param.28) | data formatting | bytes 1536 | tf_op jit(solution)/shard_map/reshape | solution.py:643
  3.1 98.1 %shard_map.222 = (bf16[32,544,128]{2,1,0:T(8,128)(2,1)}, f32[2,128,128]{2,1,0:T(8,128)}, f32[2,128,128]{2,1,0:T(8,128)}, f32[24,128]{1,0:T(8,128)}) custom-call(bf16[2,128,128]{2,1,0:T(8,128)(2,1)} %x_ref.1, bf16[2,16,640]{2,1,0:T(8,128)(2,1)} %f_ref.1, s32[2,640]{1,0:T(2,128)} %src_ref.1, s32[2,640]{1,0:T(2,128)} %tgt_ref.1, s32[2,640]{1,0:T(2,128)} %val_ref.1, ...), custom_call_target="tpu_custom_call" | custom-call | tf_op jit(solution)/shard_map/pallas_call | solution.py:612
  101.3 1.7 %slice.3.sm_ref = bf16[32,32,128]{2,1,0:T(8,128)(2,1)} slice(bf16[32,544,128]{2,1,0:T(8,128)(2,1)} %get-tuple-element.24.a_ref.b_ref), slice={[0:32], [512:544], [0:128]} | slice | bytes 524288 | tf_op jit(solution)/shard_map/slice | solution.py:649
  103.0 11.9 %shard_map.223 = (f32[128,16384]{1,0:T(8,128)}, f32[128,128]{1,0:T(8,128)}, f32[128,384]{1,0:T(8,128)}, f32[1,384]{1,0:T(1,128)}, f32[128,384]{1,0:T(8,128)}, /*...) custom-call(bf16[32,544,128]{2,1,0:T(8,128)(2,1)} %get-tuple-element, ...), custom_call_target="tpu_custom_call" | custom-call | tf_op jit(solution)/shard_map/pallas_call | solution.py:650
  114.9 1.3 %reduce = f32[384]{0:T(512)} reduce(f32[1,384]{1,0:T(1,128)} %get-tuple-element.35, f32[]{:T(128)} %constant), dimensions={0}, to_apply=%get-tuple-element.35.reduce_sub_computation | reduce | bytes 3076 | tf_op jit(solution)/shard_map/pallas_call | solution.py:650
  116.1 1.3 %reduce.1 = f32[384]{0:T(512)} reduce(f32[1,384]{1,0:T(1,128)} %get-tuple-element.37, f32[]{:T(128)} %constant), dimensions={0}, to_apply=%get-tuple-element.37.reduce_sub_computation | reduce | bytes 3076 | tf_op jit(solution)/shard_map/pallas_call | solution.py:650

commit v3 on v2

--- a/solution.py
+++ b/solution.py
@@ -13,7 +13,7 @@
 ROUND = 16
 SMALL_ROWS = 1024
 PLANE = 4
-SEMS = 128
+SEMS = 160
 
 
 def dot(a, b, ca=1, cb=0):
@@ -145,59 +145,47 @@
     def block(self, mask):
         return self.s * self.parts + self.flip(mask)
 
+    def spot(self, line):
+        return self.s * self.lines + lax.div(self.flip(line * self.plane), self.plane)
+
     def level(self, line):
         own = lax.div(self.flip(line * self.plane), self.plane) * self.plane
         return self.s * self.parts + own
 
 
-class Gather:
+class LineGather:
     def __init__(self, net, place, name, buf):
         self.net, self.place, self.name, self.buf = net, place, name, buf
 
-    def send(self, key, mask, peer):
-        ref = self.buf.at[self.place.block(mask)]
-        self.net.send((self.name,) + key, ref, ref, peer)
-
-    def recv(self, key, mask, peer):
-        self.net.wait((self.name,) + key, self.buf.at[self.place.block(mask)], peer)
+    def block(self, line):
+        return self.buf.at[self.place.spot(line)]
 
     def begin(self):
         p = self.place
         for line in range(1, p.lines):
-            self.send((line, 0), 0, p.peer(line * p.plane))
-        for q in range(1, p.plane):
-            self.send((0, q), 0, p.peer(q))
-
-    def along(self):
+            ref = self.block(0)
+            self.net.send((self.name, line), ref, ref, p.peer(line * PLANE))
+
+    def middle(self):
         p = self.place
         for line in range(1, p.lines):
-            mask = line * p.plane
-            self.recv((line, 0), mask, p.peer(mask))
-            for q in range(1, p.plane):
-                self.send((line, q), mask, p.peer(q))
-
-    def across(self):
-        p = self.place
-        for line in range(p.lines):
-            for q in range(1, p.plane):
-                self.recv((line, q), line * p.plane + q, p.peer(q))
-            ref = self.buf.at[pl.ds(p.level(line), p.plane)]
-            self.net.send((self.name, "sib", line), ref, ref, p.sibling)
+            self.net.wait((self.name, line), self.block(line), p.peer(line * PLANE))
+        ref = self.buf.at[pl.ds(p.s * p.lines, p.lines)]
+        self.net.send((self.name, "sib"), ref, ref, p.sibling)
 
     def finish(self):
         p = self.place
-        for line in range(p.lines):
-            first = p.level(line) + (1 - 2 * p.s) * p.parts
-            self.net.wait((self.name, "sib", line), self.buf.at[pl.ds(first, p.plane)], p.sibling)
+        ref = self.buf.at[pl.ds((1 - p.s) * p.lines, p.lines)]
+        self.net.wait((self.name, "sib"), ref, p.sibling)
 
 
 def main_kernel(
     x_ref, f_ref, src_ref, tgt_ref, val_ref, lab_ref, w1_ref, b1_ref, w2_hbm, b2_ref,
     wi_ref, bi_ref, wh_ref, bh_ref, cot_ref,
     full_out, states_out, grads_out, w1_out,
-    w2, amat, acc, zaug, zpre_s, hs, hsl, dms, dml, xbuf, dzacc, picks, puts,
-    ins, hid, dts, qst, tmp, mine, small, small_in, small_lo, small_line, small_plane,
-    w1_io, swap, w2_sems, own_sem, send_sems, recv_sems,
+    w2, amat, acc, zaug, zpre_s, hs, hsl, dms, dml, dzacc, picks, puts,
+    ins, hid, dts, qst, zall, part, sums, tmp, small, small_in, small_lo, small_line, small_plane,
+    w1_io, swap, w2_sems, send_sems, recv_sems,
 ):
     edges, nodes = f_ref.shape[2], x_ref.shape[1]
     tiles5 = edges // LANE
@@ -208,6 +196,8 @@
     net = Net(send_sems, recv_sems)
     s, c = place.s, place.c
     me = place.block(0)
+    here = place.spot(0)
+    group = 2 * place.lines
     rounds = LANE // ROUND
 
     barrier = pltpu.get_barrier_semaphore()
@@ -228,10 +218,13 @@
     feats = f_ref[s]
     ends = pack_ends(src_ref, tgt_ref, val_ref, lab_ref, s)
     h0 = x_ref[s]
-    table = jnp.concatenate([feats, ends.astype(BF)], axis=0)
     for e in range(tiles5):
-        ins[me, e * 32 : (e + 1) * 32, :] = table[:, e * LANE : (e + 1) * LANE]
-    ins[me, tiles5 * 32 : tiles5 * 32 + nodes, :] = h0
+        ins[here, e * 16 : (e + 1) * 16, :] = feats[:, e * LANE : (e + 1) * LANE]
+    table = [ends[q : q + 1, e * LANE : (e + 1) * LANE] for q in range(2) for e in range(tiles5)]
+    table.append(ends[2:3, :nodes])
+    table.append(jnp.zeros((16 - len(table), LANE), F32))
+    ins[here, tiles5 * 16 : (tiles5 + 1) * 16, :] = jnp.concatenate(table, axis=0).astype(BF)
+    hid[0, here] = h0
     pick, put = edge_tables(ends, nodes)
     picks[...] = pick
     puts[...] = put
@@ -250,12 +243,11 @@
     b2t = b2_ref[...].T
     tiles = [(e, min(256, edges - e)) for e in range(0, edges, 256)]
 
-    pl.semaphore_wait(barrier, len(peers))
-    gather_in = Gather(net, place, "in", ins)
-    gather_h1 = Gather(net, place, "h1", hid)
-    gather_d2 = Gather(net, place, "d2", dts.at[1])
-    gather_d1 = Gather(net, place, "d1", dts.at[0])
-    gather_in.begin()
+    gather_in = LineGather(net, place, "in", ins)
+    gather_h0 = LineGather(net, place, "h0", hid.at[0])
+    gather_h1 = LineGather(net, place, "h1", hid.at[1])
+    gather_d2 = LineGather(net, place, "d2", dts.at[1])
+    gather_d1 = LineGather(net, place, "d1", dts.at[0])
 
     def keep(i, e, w, p):
         p = p.reshape(16, 8, w).sum(0)
@@ -277,8 +269,11 @@
                 p = a[v * LANE : (v + 1) * LANE].astype(F32) * hs[0, :, e : e + w]
                 keep(ib * ROUND + v, e, w, p)
 
-    loop(rounds, first)
-    gather_in.along()
+    loop(rounds - 2, first)
+    pl.semaphore_wait(barrier, len(peers))
+    gather_in.begin()
+    gather_h0.begin()
+    loop(2, lambda ib: first(ib + rounds - 2))
 
     def again(ib):
         for e, w in tiles:
@@ -299,16 +294,16 @@
             total = total + dot(puts[...], piece, 1, 1)
         return total.astype(BF)
 
-    weights = (wi_ref[...], bi_ref[...], wh_ref[...], bh_ref[...])
+    weights = (wi_ref[...], bi_ref[...].reshape(1, -1), wh_ref[...], bh_ref[...].reshape(1, -1))
     m1 = gathered()
     gates1 = gru_forward(m1, h0, *weights)
     h1 = gates1[0].astype(BF)
-    hid[me] = h1
+    hid[1, here] = h1
     gather_h1.begin()
     sources(1, h1)
     loop(LANE // 8, again)
-    gather_in.across()
-    gather_h1.along()
+    gather_in.middle()
+    gather_h0.middle()
     m2 = gathered()
     gates2 = gru_forward(m2, h1, *weights)
     h2 = gates2[0]
@@ -316,7 +311,7 @@
     g2 = cot_ref[s] * label
     dgi2, dgh2, dm2, dh2 = gru_backward(g2, h1, gates2, weights[0], weights[2])
     dt2 = dm2.T
-    dts[1, me] = dt2
+    dts[1, here] = dt2
     gather_d2.begin()
 
     def spread(t, dt):
@@ -343,13 +338,95 @@
 
     spread(1, dt2)
     back2 = [to_source_tile(1, e) for e in range(tiles5)]
-    gather_d2.along()
-    gather_h1.across()
+    gather_h1.middle()
     d1 = (dh2 + to_nodes(back2)).astype(BF)
     dgi1, dgh1, dm1, dh1 = gru_backward(d1.astype(F32), h0, gates1, weights[0], weights[2])
     dt1 = dm1.T
-    dts[0, me] = dt1
+    dts[0, here] = dt1
     gather_d1.begin()
+    gather_d2.middle()
+
+    gather_in.finish()
+    gather_h0.finish()
+    gather_h1.finish()
+    dzacc[...] = jnp.zeros_like(dzacc)
+
+    def back_hidden(ib):
+        total = dzacc[...]
+        for a in range(2):
+            for t in range(2):
+                h = hsl[:, t * edges : (t + 1) * edges].astype(F32)
+                d = dms[t, aligned(ib * 2 + a, 8), :]
+                for v in range(8):
+                    qst[a, v * LANE : (v + 1) * LANE, t * edges : (t + 1) * edges] = (
+                        h * d[v : v + 1]
+                    ).astype(BF)
+            total = total + dot(w2[:, aligned(ib * 2 + a, 8 * LANE)], qst[a, :, 0 : 2 * edges])
+        dzacc[...] = total
+
+    units = PLANE * per
+    ks = lax.broadcasted_iota(jnp.int32, (units, LANE), 0)
+    ks = (lax.div(ks, per) * 2 + s) * per + lax.rem(ks, per) + lax.div(c, PLANE) * (2 * units)
+    sel = (ks == lax.broadcasted_iota(jnp.int32, (units, LANE), 1)).astype(F32)
+    w1t = dot(sel.astype(BF), w1_ref[...], 1, 1).astype(BF)
+    b1 = jnp.sum(sel * b1_ref[...].astype(F32), axis=1, keepdims=True)
+    quarter = nodes // 4
+    qn = lax.broadcasted_iota(jnp.int32, (quarter, 256), 0).astype(F32)
+    sn = lax.broadcasted_iota(jnp.int32, (nodes, 256), 0).astype(F32)
+
+    def hidden(blk):
+        cols = [ins[blk, e * 16 : (e + 1) * 16, :] for e in range(tiles5)]
+        z = jax.nn.silu(dot(w1t, jnp.concatenate(cols, axis=1)) + b1)
+        zall[blk] = z.astype(BF).astype(F32)
+
+    def build(blk):
+        z = zall[blk]
+        en = ins[blk, tiles5 * 16 : (tiles5 + 1) * 16, :].astype(F32)
+        pairs = []
+        for q in range(4):
+            lo = q * LANE
+            zq = z[:, lo : lo + 256]
+            src = jnp.concatenate([en[q : q + 1], en[q + 1 : q + 2]], axis=1)
+            tgt = jnp.concatenate(
+                [en[tiles5 + q : tiles5 + q + 1], en[tiles5 + q + 1 : tiles5 + q + 2]], axis=1
+            )
+            hit_t = (qn + float(q * quarter)) == tgt
+            hit_s = (sn == src).astype(F32).astype(BF)
+            lhs = [jnp.where(hit_t, zq[k : k + 1], 0.0).astype(BF) for k in range(units)]
+            pairs.append(dot(jnp.concatenate(lhs, axis=0), hit_s, 1, 1))
+        pairs = jnp.concatenate(split(jnp.concatenate(pairs, axis=0), 2), axis=1)
+        h = jnp.concatenate([hid[0, blk], hid[1, blk]], axis=1)
+        got = dot(pairs, jnp.concatenate([h, h], axis=0)).astype(BF)
+        for q in range(4):
+            at = pl.ds(pl.multiple_of(blk * nodes + q * quarter, quarter), quarter)
+            for k in range(units):
+                part = got[(q * units + k) * quarter : (q * units + k + 1) * quarter]
+                for t in range(2):
+                    qst[t, at, k * LANE : (k + 1) * LANE] = part[:, t * LANE : (t + 1) * LANE]
+
+    for blk in range(group):
+        hidden(blk)
+    loop(group, build)
+    gather_d1.middle()
+    gather_d2.finish()
+    lhs = jnp.concatenate([dts[1, blk] for blk in range(group)], axis=1)
+    part[...] = dot(lhs, qst[1])
+    gather_d1.finish()
+    lhs = jnp.concatenate([dts[0, blk] for blk in range(group)], axis=1)
+    part[...] += dot(lhs, qst[0])
+    count = jnp.zeros((1, LANE), F32)
+    for blk in range(group):
+        count = count + ins[blk, tiles5 * 16 : (tiles5 + 1) * 16, :].astype(F32)[10:11]
+    count = jnp.concatenate([count, jnp.zeros((15, LANE), F32)], axis=0)
+    for p in range(PLANE):
+        for k in range(per):
+            col = (p * per + k) * LANE
+            tmp[pl.ds(k, LANE, stride=per), :] = part[:, col : col + LANE]
+        sums[0, p, 0 : per * LANE] = tmp[...].astype(BF)
+        sums[0, p, per * LANE :] = count.astype(BF)
+    for q in range(1, PLANE):
+        to = lax.rem(place.flip(q), PLANE)
+        net.send(("sums", q), sums.at[0, to], sums.at[1, q], place.peer(q))
 
     half = SMALL_ROWS // 2
     plane_rows = half // place.lines
@@ -368,9 +445,7 @@
     small[7 * LANE :] = jnp.concatenate(rows, axis=0)
     net.send(("small", "sib"), small.at[aligned(1 - s, half)], small_in, place.sibling)
 
-    back1 = [to_source_tile(0, e) for e in range(3)]
-    gather_d1.along()
-    gather_d2.across()
+    back1 = [to_source_tile(0, e) for e in range(2)]
     net.wait(("small", "sib"), small_in, place.sibling)
     small_lo[...] = (small[aligned(s, half), :] + small_in[...]).astype(BF)
     z = lax.div(c, PLANE)
@@ -382,58 +457,7 @@
             small_line.at[line],
             place.peer(line * PLANE),
         )
-    back1 += [to_source_tile(0, e) for e in range(3, tiles5)]
-    d0 = dh1 + to_nodes(back1)
-    gather_in.finish()
-    gather_h1.finish()
-
-    zero = s == 0
-    swap[0, 0] = jnp.where(zero, h2, h1.astype(F32))
-    swap[0, 1] = jnp.where(zero, d1.astype(F32), d0)
-    net.send(("swap",), swap.at[0], swap.at[1], place.sibling)
-
-    first_k = (c * 2 + s) * per
-    ks = lax.broadcasted_iota(jnp.int32, (8, LANE), 0) + first_k
-    sel = (ks == lax.broadcasted_iota(jnp.int32, (8, LANE), 1)).astype(F32)
-    w1t = dot(sel.astype(BF), w1_ref[...], 1, 1).astype(BF)
-    b1 = jnp.sum(sel * b1_ref[...].astype(F32), axis=1, keepdims=True)
-    quarter = nodes // 4
-    qn = lax.broadcasted_iota(jnp.int32, (quarter, 256), 0).astype(F32)
-    sn = lax.broadcasted_iota(jnp.int32, (nodes, 256), 0).astype(F32)
-
-    def build(blk):
-        cols = [ins[blk, e * 32 : (e + 1) * 32, :] for e in range(tiles5)]
-        fi = jnp.concatenate(cols, axis=1)
-        z = jax.nn.silu(dot(w1t, fi[0:16]) + b1).astype(BF).astype(F32)
-        en = fi[16:32].astype(F32)
-        pairs = []
-        for q in range(4):
-            lo = q * LANE
-            zq = z[:, lo : lo + 256]
-            hit_t = (qn + float(q * quarter)) == en[1:2, lo : lo + 256]
-            hit_s = (sn == en[0:1, lo : lo + 256]).astype(F32).astype(BF)
-            lhs = [jnp.where(hit_t, zq[k : k + 1], 0.0).astype(BF) for k in range(per)]
-            pairs.append(dot(jnp.concatenate(lhs, axis=0), hit_s, 1, 1))
-        pairs = jnp.concatenate(split(jnp.concatenate(pairs, axis=0), 2), axis=1)
-        h = jnp.concatenate([ins[blk, tiles5 * 32 : tiles5 * 32 + nodes, :], hid[blk]], axis=1)
-        got = dot(pairs, jnp.concatenate([h, h], axis=0)).astype(BF)
-        for q in range(4):
-            at = pl.ds(pl.multiple_of(blk * nodes + q * quarter, quarter), quarter)
-            for k in range(per):
-                part = got[(q * per + k) * quarter : (q * per + k + 1) * quarter]
-                for t in range(2):
-                    qst[t, at, k * LANE : (k + 1) * LANE] = part[:, t * LANE : (t + 1) * LANE]
-
-    loop(blocks, build)
-    gather_d1.across()
-    gather_d2.finish()
-    lhs = jnp.concatenate([dts[1, blk] for blk in range(blocks)], axis=1)
-    total = dot(lhs, qst[1])
-    count = jnp.zeros((1, LANE), F32)
-    for blk in range(blocks):
-        count = count + ins[blk, 16:32, :].astype(F32)[2:3]
-    scale = 1.0 / jnp.sum(count, axis=1, keepdims=True)
-
+    back1.append(to_source_tile(0, 2))
     own = small_lo[aligned(z, plane_rows), :].astype(F32)
     for line in range(1, place.lines):
         net.wait(("small", "line", line), small_line.at[line], place.peer(line * PLANE))
@@ -448,44 +472,59 @@
             small_plane.at[q],
             place.peer(q),
         )
-    gather_d1.finish()
-    lhs = jnp.concatenate([dts[0, blk] for blk in range(blocks)], axis=1)
-    total = (total + dot(lhs, qst[0])) * scale
-    for k in range(per):
-        tmp[pl.ds(k, LANE, stride=per), :] = total[:, k * LANE : (k + 1) * LANE]
-    mine[0 : per * LANE] = tmp[...].astype(BF)
+    total = sums[0, q_me].astype(F32)
+    for q in range(1, PLANE):
+        net.wait(("sums", q), sums.at[1, q], place.peer(q))
+        total = total + sums[1, q].astype(F32)
+    scale = 1.0 / jnp.sum(total[per * LANE : per * LANE + 1], axis=1, keepdims=True)
+    full_out[me, 0 : per * LANE] = (total[0 : per * LANE] * scale).astype(BF)
+
+    size = full_out.shape[1]
+    mine = full_out.at[me]
+    tail = size // 5 // 16 * 16
+    cut = (size - tail) // 32 * 16
+    halves = (pl.ds(0, cut), pl.ds(cut, size - tail - cut))
+    head, last = pl.ds(0, size - tail), pl.ds(size - tail, tail)
+    net.send(("out", 1), mine.at[head], full_out.at[me, head], place.peer(PLANE))
+    for q, a in ((1, 0), (2, 1), (1, 1), (2, 0)):
+        net.send(("out", 0, q, a), mine.at[halves[a]], full_out.at[me, halves[a]], place.peer(q))
+    for line in range(2, place.lines):
+        net.send(("out", line), mine.at[head], full_out.at[me, head], place.peer(line * PLANE))
+    back1 += [to_source_tile(0, e) for e in range(3, tiles5)]
+    d0 = dh1 + to_nodes(back1)
+
+    zero = s == 0
+    swap[0, 0] = jnp.where(zero, h2, h1.astype(F32))
+    swap[0, 1] = jnp.where(zero, d1.astype(F32), d0)
+    net.send(("swap",), swap.at[0], swap.at[1], place.sibling)
     own = small_line[0, aligned(q_me, own_rows), :].astype(F32)
     for q in range(1, PLANE):
         net.wait(("small", "plane", q), small_plane.at[q], place.peer(q))
         own = own + small_plane[q].astype(F32)
-    mine[per * LANE : per * LANE + own_rows] = (own * scale).astype(BF)
-
-    size = mine.shape[0]
-    halves = (pl.ds(0, size // 2), pl.ds(size // 2, size // 2))
-    keep_own = pltpu.make_async_copy(mine, full_out.at[me], own_sem)
-    keep_own.start()
-    for line in range(1, place.lines):
-        net.send(("out", line), mine, full_out.at[me], place.peer(line * PLANE))
-    for q in (1, 2):
-        for a in range(2):
-            net.send(
-                ("out", 0, q, a), mine.at[halves[a]], full_out.at[me, halves[a]], place.peer(q)
-            )
+    full_out[me, per * LANE : per * LANE + own_rows] = (own * scale).astype(BF)
+    for q in range(1, PLANE):
+        net.send(("last", 0, q), mine.at[last], full_out.at[me, last], place.peer(q))
 
     def out_line(line):
         mask = line * PLANE
         blk = place.block(mask)
-        net.wait(("out", line), full_out.at[blk], place.peer(mask))
-        for q in (1, 2):
-            for a in range(2):
-                ref = full_out.at[blk, halves[a]]
-                net.send(("out", line, q, a), ref, ref, place.peer(q))
+        net.wait(("out", line), full_out.at[blk, head], place.peer(mask))
+        for q, a in ((1, 0), (2, 1), (1, 1), (2, 0)):
+            ref = full_out.at[blk, halves[a]]
+            net.send(("out", line, q, a), ref, ref, place.peer(q))
 
     def out_cross(line):
         for q, a in ((1, 0), (2, 1)):
             ref = full_out.at[place.block(line * PLANE + q), halves[a]]
             net.wait(("out", line, q, a), ref, place.peer(q))
             net.send(("out", line, 3, a), ref, ref, place.peer(3 - q))
+
+    def last_lines():
+        for q in range(1, PLANE):
+            net.wait(("last", 0, q), full_out.at[place.block(q), last], place.peer(q))
+        ref = full_out.at[pl.ds(place.level(0), PLANE), last]
+        for line in range(1, place.lines):
+            net.send(("last", line), ref, ref, place.peer(line * PLANE))
 
     def out_level(line):
         for q, a in ((1, 1), (2, 0)):
@@ -495,29 +534,17 @@
             ref = full_out.at[place.block(line * PLANE + 3), halves[a]]
             net.wait(("out", line, 3, a), ref, place.peer(q))
         ref = full_out.at[pl.ds(place.level(line), PLANE)]
+        if line > 0:
+            part = full_out.at[pl.ds(place.level(line), PLANE), last]
+            net.wait(("last", line), part, place.peer(line * PLANE))
         net.send(("out", "sib", line), ref, ref, place.sibling)
 
-    dzacc[...] = jnp.zeros_like(dzacc)
-
-    def back_hidden(ib):
-        for t in range(2):
-            h = hsl[:, t * edges : (t + 1) * edges].astype(F32)
-            d = dms[t, aligned(ib, ROUND), :]
-            for v in range(ROUND):
-                xbuf[v * LANE : (v + 1) * LANE, t * edges : (t + 1) * edges] = (
-                    h * d[v : v + 1]
-                ).astype(BF)
-        dzacc[...] += dot(w2[:, aligned(ib, ROUND * LANE)], xbuf[...])
-
-    loop(rounds // 4, back_hidden)
-    for line in range(1, place.lines):
-        out_line(line)
-    loop(rounds // 2, lambda ib: back_hidden(ib + rounds // 4))
-    keep_own.wait()
-    for line in range(place.lines):
-        out_cross(line)
-    loop(rounds // 4, lambda ib: back_hidden(ib + 3 * rounds // 4))
-
+    loop(3, back_hidden)
+    out_cross(0)
+    loop(2, lambda ib: back_hidden(ib + 3))
+    out_line(1)
+    last_lines()
+    loop(rounds - 5, lambda ib: back_hidden(ib + 5))
     zp = zpre_s[...]
     sig = jax.nn.sigmoid(zp)
     slope = sig * (1.0 + zp * (1.0 - sig))
@@ -530,12 +557,24 @@
         total = total + dot(lhs, dzpre, 1, 1)
     w1_io[0] = total[0:24]
     net.send(("w1", "sib"), w1_io.at[0], w1_io.at[1], place.sibling)
+    out_cross(1)
+    out_level(0)
     net.wait(("w1", "sib"), w1_io.at[1], place.sibling)
     total = w1_io[0] + w1_io[1]
     w1_io[2] = total
     at = 4
     for line in range(1, place.lines):
         net.send(("w1", "line", line), w1_io.at[2], w1_io.at[at + line], place.peer(line * PLANE))
+    net.wait(("swap",), swap.at[1], place.sibling)
+    mine_state = jnp.where(zero, h1.astype(F32), h2)
+    mine_grad = jnp.where(zero, d0, d1.astype(F32))
+    states_out[0] = jnp.where(zero, mine_state, swap[1, 0])
+    states_out[1] = jnp.where(zero, swap[1, 0], mine_state)
+    grads_out[0] = jnp.where(zero, mine_grad, swap[1, 1])
+    grads_out[1] = jnp.where(zero, swap[1, 1], mine_grad)
+    for line in range(2, place.lines):
+        out_line(line)
+    out_level(1)
     for line in range(1, place.lines):
         net.wait(("w1", "line", line), w1_io.at[at + line], place.peer(line * PLANE))
         total = total + w1_io[at + line]
@@ -543,19 +582,13 @@
     at += place.lines
     for q in range(1, PLANE):
         net.send(("w1", "plane", q), w1_io.at[3], w1_io.at[at + q], place.peer(q))
+    for line in range(2, place.lines):
+        out_cross(line)
     for q in range(1, PLANE):
         net.wait(("w1", "plane", q), w1_io.at[at + q], place.peer(q))
         total = total + w1_io[at + q]
     w1_out[...] = total * scale
-
-    net.wait(("swap",), swap.at[1], place.sibling)
-    mine_state = jnp.where(zero, h1.astype(F32), h2)
-    mine_grad = jnp.where(zero, d0, d1.astype(F32))
-    states_out[0] = jnp.where(zero, mine_state, swap[1, 0])
-    states_out[1] = jnp.where(zero, swap[1, 0], mine_state)
-    grads_out[0] = jnp.where(zero, mine_grad, swap[1, 1])
-    grads_out[1] = jnp.where(zero, swap[1, 1], mine_grad)
-    for line in range(place.lines):
+    for line in range(2, place.lines):
         out_level(line)
     for line in range(place.lines):
         first = place.level(line) + (1 - 2 * s) * parts
@@ -563,33 +596,43 @@
     net.drain()
 
 
-def final_kernel(a_ref, b_ref, sm_ref, w1_ref, st_ref, sg_ref, w2_out, b2_out, wi_out, bi_out,
-                 wh_out, bh_out, gw1_out, gb1_out, st_out, sg_out):
+def final_kernel(full_ref, w1_ref, st_ref, sg_ref, w2_out, b2_out, wi_out, bi_out, wh_out, bh_out,
+                 gw1_out, gb1_out, st_out, sg_out, flat, out_sems):
+    blocks = full_ref.shape[0]
+    parts = blocks // 2
+    width = b2_out.shape[0]
+    rows = width * (width // blocks)
+
+    def put(c):
+        part = aligned(c, 8)
+        return pltpu.make_async_copy(flat.at[part], w2_out.at[part], out_sems.at[c])
+
+    gw1_out[...] = w1_ref[0:16]
+    gb1_out[...] = w1_ref[16:17]
+    st_out[...] = st_ref[...]
+    sg_out[...] = sg_ref[...]
     low = lax.broadcasted_iota(jnp.int32, (1, 8, LANE), 1) < 4
-    rows = b2_out.shape[0] * 4
-    a = a_ref[0, :rows].astype(F32).reshape(rows // 8, 8, LANE)
-    b = b_ref[0, :rows].astype(F32).reshape(rows // 8, 8, LANE)
-    even = jnp.where(low, a, pltpu.roll(b, 4, 1))
-    odd = jnp.where(low, pltpu.roll(a, 4, 1), b)
-    for p in range(rows // 8):
-        w2_out[:, (2 * p) * LANE : (2 * p + 1) * LANE] = even[p]
-        w2_out[:, (2 * p + 1) * LANE : (2 * p + 2) * LANE] = odd[p]
-
-    @pl.when(pl.program_id(0) == 0)
-    def _():
-        own = sm_ref.shape[1]
-        x = sm_ref[...].astype(F32).reshape(-1, LANE)
-        for q in range(3):
-            cols = slice(q * LANE, (q + 1) * LANE)
-            wi_out[:, cols] = x[q * LANE : (q + 1) * LANE]
-            wh_out[:, cols] = x[(3 + q) * LANE : (4 + q) * LANE]
-            bi_out[:, cols] = x[7 * LANE + q : 7 * LANE + q + 1]
-            bh_out[:, cols] = x[7 * LANE + 3 + q : 7 * LANE + 4 + q]
-        b2_out[...] = x[6 * LANE : 7 * LANE]
-        gw1_out[...] = w1_ref[0:16]
-        gb1_out[...] = w1_ref[16:17]
-        st_out[...] = st_ref[...]
-        sg_out[...] = sg_ref[...]
+
+    def place_rows(c):
+        a = full_ref[c, :rows].astype(F32).reshape(rows // 8, 8, LANE)
+        b = full_ref[c + parts, :rows].astype(F32).reshape(rows // 8, 8, LANE)
+        even = jnp.where(low, a, pltpu.roll(b, 4, 1))
+        odd = jnp.where(low, pltpu.roll(a, 4, 1), b)
+        for p in range(rows // 8):
+            flat[aligned(c, 8), (2 * p) * LANE : (2 * p + 1) * LANE] = even[p]
+            flat[aligned(c, 8), (2 * p + 1) * LANE : (2 * p + 2) * LANE] = odd[p]
+        put(c).start()
+
+    loop(parts, place_rows)
+    x = full_ref[:, rows:].astype(F32).reshape(-1, LANE)
+    for q in range(3):
+        cols = slice(q * LANE, (q + 1) * LANE)
+        wi_out[:, cols] = x[q * LANE : (q + 1) * LANE]
+        wh_out[:, cols] = x[(3 + q) * LANE : (4 + q) * LANE]
+        bi_out[cols] = x[7 * LANE + q]
+        bh_out[cols] = x[7 * LANE + 3 + q]
+    b2_out[...] = x[6 * LANE : 7 * LANE]
+    loop(parts, lambda c: put(c).wait())
 
 
 def shards(
@@ -602,6 +645,7 @@
     blocks = 2 * parts
     per = width // blocks
     lines = parts // PLANE
+    group, units = 2 * lines, PLANE * per
     half = SMALL_ROWS // 2
     plane_rows = half // lines
     own_rows = plane_rows // PLANE
@@ -612,67 +656,58 @@
     full, states, grads, gw1 = pl.pallas_call(
         main_kernel,
         out_shape=(
-            sds((blocks, size, width), BF), sds((2, nodes, width), F32),
-            sds((2, nodes, width), F32), sds((24, width), F32),
+            VMEM((blocks, size, width), BF), VMEM((2, nodes, width), F32),
+            VMEM((2, nodes, width), F32), VMEM((24, width), F32),
         ),
         in_specs=[vm] * 8 + [hbm] + [vm] * 6,
-        out_specs=[hbm, vm, vm, vm],
+        out_specs=[vm] * 4,
         scratch_shapes=[
             VMEM((width, width * width), BF), VMEM((width * width, edges), BF),
             VMEM((edges // LANE, 8 * width, LANE), F32), VMEM((2 * width, edges), BF),
             VMEM((width, edges), F32), VMEM((2, width, edges), F32),
             VMEM((width, 2 * edges), BF), VMEM((2, width, edges), F32),
-            VMEM((width, 2 * edges), BF), VMEM((ROUND * width, 2 * edges), BF),
+            VMEM((width, 2 * edges), BF),
             VMEM((width, 2 * edges), F32), VMEM((nodes, edges), BF), VMEM((nodes, edges), BF),
-            VMEM((blocks, 32 * (edges // LANE) + nodes, LANE), BF),
-            VMEM((blocks, nodes, width), BF), VMEM((2, blocks, width, nodes), BF),
-            VMEM((2, blocks * nodes, per * width), BF), VMEM((width * per, width), F32),
-            VMEM((size, width), BF), VMEM((SMALL_ROWS, width), F32), VMEM((half, width), F32),
+            VMEM((group, 16 * (edges // LANE + 1), LANE), BF),
+            VMEM((2, group, nodes, width), BF), VMEM((2, group, width, nodes), BF),
+            VMEM((2, group * nodes, units * width), BF), VMEM((group, units, edges), F32),
+            VMEM((width, units * width), F32),
+            VMEM((2, PLANE, per * width + 16, width), BF), VMEM((width * per, width), F32),
+            VMEM((SMALL_ROWS, width), F32), VMEM((half, width), F32),
             VMEM((half, width), BF), VMEM((lines, plane_rows, width), BF),
             VMEM((PLANE, own_rows, width), BF), VMEM((4 + lines + PLANE, 24, width), F32),
             VMEM((2, 2, nodes, width), F32),
-            pltpu.SemaphoreType.DMA((width // ROUND,)), pltpu.SemaphoreType.DMA,
+            pltpu.SemaphoreType.DMA((width // ROUND,)),
             pltpu.SemaphoreType.DMA((SEMS,)), pltpu.SemaphoreType.DMA((SEMS,)),
         ],
         compiler_params=pltpu.CompilerParams(
-            collective_id=0, has_side_effects=True, vmem_limit_bytes=62 * 2**20
+            collective_id=0, has_side_effects=True, vmem_limit_bytes=57 * 2**20
         ),
     )(
         node_input, edge_input, edge_source, edge_target, edge_valid, node_labeled,
         edge_w1, edge_b1.reshape(1, -1), edge_w2, edge_b2.reshape(width, width),
-        gru_wi, gru_bi.reshape(1, -1), gru_wh, gru_bh.reshape(1, -1), state_cot,
-    )
-
-    def whole(*shape):
-        return pl.BlockSpec(shape, lambda c: (0,) * len(shape))
-
-    small = full[:, width * per :, :]
+        gru_wi, gru_bi, gru_wh, gru_bh, state_cot,
+    )
+
     w2, b2, wi, bi, wh, bh, w1, b1, states, grads = pl.pallas_call(
         final_kernel,
-        grid=(parts,),
         out_shape=(
             sds((width, width * width), F32), sds((width, width), F32),
-            sds((width, 3 * width), F32), sds((1, 3 * width), F32),
-            sds((width, 3 * width), F32), sds((1, 3 * width), F32),
+            sds((width, 3 * width), F32), sds((3 * width,), F32),
+            sds((width, 3 * width), F32), sds((3 * width,), F32),
             sds((16, width), F32), sds((1, width), F32),
             sds((2, nodes, width), F32), sds((2, nodes, width), F32),
         ),
-        in_specs=[
-            pl.BlockSpec((1, size, width), lambda c: (c, 0, 0)),
-            pl.BlockSpec((1, size, width), lambda c: (c + parts, 0, 0)),
-            whole(blocks, own_rows, width), whole(24, width),
-            whole(2, nodes, width), whole(2, nodes, width),
+        in_specs=[vm] * 4,
+        out_specs=[hbm] + [vm] * 9,
+        scratch_shapes=[
+            VMEM((width, width * width), F32), pltpu.SemaphoreType.DMA((parts,)),
         ],
-        out_specs=(
-            pl.BlockSpec((2 * per, width * width), lambda c: (c, 0)), whole(width, width),
-            whole(width, 3 * width), whole(1, 3 * width), whole(width, 3 * width),
-            whole(1, 3 * width), whole(16, width), whole(1, width),
-            whole(2, nodes, width), whole(2, nodes, width),
-        ),
-    )(full, full, small, gw1, states, grads)
+        compiler_params=pltpu.CompilerParams(vmem_limit_bytes=40 * 2**20),
+    )(full, gw1, states, grads)
     return (
         states[None], grads[None], w1, b1.reshape(-1), w2, b2.reshape(-1),
-        wi, bi.reshape(-1), wh, bh.reshape(-1),
+        wi, bi, wh, bh,
     )
 
 

time: 118 us -> 79 us (0.67)
  Pallas kernels: 110 us -> 78.2 us
  local copies, waits for them, and re-layouts: 4.16 us -> 0 us
  other arithmetic: 2.53 us -> 0 us
    pallas_call x2, Pallas kernels: 110 us -> 78.2 us  [the longest x1 73.8 us: shards(): pl.pallas_call(main_kernel, out_shape=(VMEM((blocks, size, width), BF), V...]
    pallas_call x2 -> x0, other arithmetic: 2.53 us -> none  [shards(): pl.pallas_call(final_kernel, grid=(parts,), out_shape=(sds((width, width...]
    reshape x2 -> x0, local copies, waits for them, and re-layouts: 2.49 us -> none  [the longest x1 1.24 us: shards(): gru_bi.reshape(1, -1)]
    slice x1 -> x0, local copies, waits for them, and re-layouts: 1.67 us -> none  [shards(): small = full[:, width * per:, :]]
where the time goes in v3:
time: 79 us; the launch traced here: 78.8 us
  Pallas kernels  78.2 us (99%)
    pallas_call x1, Pallas kernels, shards(): pl.pallas_call(main_kernel, out_shape=(VMEM((blocks, size, width), BF), V...  73.8 us
    pallas_call x1, Pallas kernels, shards(): pl.pallas_call(final_kernel, out_shape=(sds((width, width * width), F32),...  4.35 us

profile of v3, /device:TPU:0, one launch (start us, length us, event | category | flops | bytes accessed | tf_op | source)
XLA Modules:
  0.0 78.8 jit_solution(7672000507653820515)
XLA Ops:
  0.6 73.8 %shard_map.222 = (bf16[32,544,128]{2,1,0:T(8,128)(2,1)S(1)}, f32[2,128,128]{2,1,0:T(8,128)S(1)}, f32[2,128,128]{2,1,0:T(8,128)S(1)}, f32[24,128]{1,0:T(8,128)S(1)}) custom-call(bf16[2,128,128]{2,1,0:T(8,128)(2,1)} %x_ref.1, bf16[2,16,640]{2,1,0:T(8,128)(2,1)} %f_ref.1, s32[2,640]{1,0:T(2,128)} %src_ref.1, s32[2,640]{1,0:T(2,128)} %tgt_ref.1, ...), custom_call_target="tpu_custom_call" | custom-call | tf_op jit(solution)/shard_map/pallas_call | solution.py:656
  74.5 4.4 %shard_map.223 = (f32[128,16384]{1,0:T(8,128)}, f32[128,128]{1,0:T(8,128)}, f32[128,384]{1,0:T(8,128)}, f32[384]{0:T(512)}, f32[128,384]{1,0:T(8,128)}, /*index=...) custom-call(bf16[32,544,128]{2,1,0:T(8,128)(2,1)S(1)} %get-tuple-element.24.f, ...), custom_call_target="tpu_custom_call" | custom-call | tf_op jit(solution)/shard_map/pallas_call | solution.py:692

commit v4 on v3

--- a/solution.py
+++ b/solution.py
@@ -10,7 +10,7 @@
 BF, F32 = jnp.bfloat16, jnp.float32
 VMEM = pltpu.VMEM
 LANE = 128
-ROUND = 16
+ROUND = 32
 SMALL_ROWS = 1024
 PLANE = 4
 SEMS = 160
@@ -92,7 +92,7 @@
 class Net:
     def __init__(self, send_sems, recv_sems):
         self.send_sems, self.recv_sems = send_sems, recv_sems
-        self.slots, self.sent = {}, []
+        self.slots, self.sent, self.settled = {}, [], 0
 
     def slot(self, key):
         return self.slots.setdefault(key, len(self.slots))
@@ -120,8 +120,12 @@
         ).wait_recv()
 
     def drain(self):
-        for copy in self.sent:
+        self.settle(len(self.sent))
+
+    def settle(self, count):
+        for copy in self.sent[self.settled : count]:
             copy.wait_send()
+        self.settled = max(self.settled, count)
 
 
 class Place:
@@ -269,11 +273,11 @@
                 p = a[v * LANE : (v + 1) * LANE].astype(F32) * hs[0, :, e : e + w]
                 keep(ib * ROUND + v, e, w, p)
 
-    loop(rounds - 2, first)
+    loop(rounds // 2, first)
     pl.semaphore_wait(barrier, len(peers))
     gather_in.begin()
     gather_h0.begin()
-    loop(2, lambda ib: first(ib + rounds - 2))
+    loop(rounds - rounds // 2, lambda ib: first(ib + rounds // 2))
 
     def again(ib):
         for e, w in tiles:
@@ -302,8 +306,6 @@
     gather_h1.begin()
     sources(1, h1)
     loop(LANE // 8, again)
-    gather_in.middle()
-    gather_h0.middle()
     m2 = gathered()
     gates2 = gru_forward(m2, h1, *weights)
     h2 = gates2[0]
@@ -338,6 +340,8 @@
 
     spread(1, dt2)
     back2 = [to_source_tile(1, e) for e in range(tiles5)]
+    gather_in.middle()
+    gather_h0.middle()
     gather_h1.middle()
     d1 = (dh2 + to_nodes(back2)).astype(BF)
     dgi1, dgh1, dm1, dh1 = gru_backward(d1.astype(F32), h0, gates1, weights[0], weights[2])
@@ -354,14 +358,11 @@
     def back_hidden(ib):
         total = dzacc[...]
         for a in range(2):
-            for t in range(2):
-                h = hsl[:, t * edges : (t + 1) * edges].astype(F32)
-                d = dms[t, aligned(ib * 2 + a, 8), :]
-                for v in range(8):
-                    qst[a, v * LANE : (v + 1) * LANE, t * edges : (t + 1) * edges] = (
-                        h * d[v : v + 1]
-                    ).astype(BF)
-            total = total + dot(w2[:, aligned(ib * 2 + a, 8 * LANE)], qst[a, :, 0 : 2 * edges])
+            d = [dms[t, aligned(ib * 2 + a, 8), :] for t in range(2)]
+            for v in range(8):
+                both = hs[0] * d[0][v : v + 1] + hs[1] * d[1][v : v + 1]
+                qst[a, v * LANE : (v + 1) * LANE, 0:edges] = both.astype(BF)
+            total = total + dot(w2[:, aligned(ib * 2 + a, 8 * LANE)], qst[a, :, 0:edges])
         dzacc[...] = total
 
     units = PLANE * per
@@ -411,22 +412,39 @@
     gather_d2.finish()
     lhs = jnp.concatenate([dts[1, blk] for blk in range(group)], axis=1)
     part[...] = dot(lhs, qst[1])
-    gather_d1.finish()
-    lhs = jnp.concatenate([dts[0, blk] for blk in range(group)], axis=1)
-    part[...] += dot(lhs, qst[0])
     count = jnp.zeros((1, LANE), F32)
     for blk in range(group):
         count = count + ins[blk, tiles5 * 16 : (tiles5 + 1) * 16, :].astype(F32)[10:11]
-    count = jnp.concatenate([count, jnp.zeros((15, LANE), F32)], axis=0)
-    for p in range(PLANE):
+    count = jnp.concatenate([count, jnp.zeros((15, LANE), F32)], axis=0).astype(BF)
+    mid = per * LANE // 2
+    early = len(net.sent)
+    pieces = (pl.ds(0, 16 + mid), pl.ds(16 + mid, per * LANE - mid))
+
+    def send_sums(ch, q):
+        ref = sums.at[0, lax.rem(place.flip(q), PLANE), pieces[ch]]
+        net.send(("sums", ch, q), ref, sums.at[1, q, pieces[ch]], place.peer(q))
+
+    def add_sums(ch):
+        total = sums[0, q_me, pieces[ch], :].astype(F32)
+        for q in range(1, PLANE):
+            net.wait(("sums", ch, q), sums.at[1, q, pieces[ch]], place.peer(q))
+            total = total + sums[1, q, pieces[ch], :].astype(F32)
+        return total
+
+    gather_d1.finish()
+    lhs = jnp.concatenate([dts[0, blk] for blk in range(group)], axis=1)
+    for q in (3, 1, 2, 0):
+        to = lax.rem(place.flip(q), PLANE)
+        cols = aligned(to, per * LANE)
+        got = part[:, cols] + dot(lhs, qst[0, :, cols])
         for k in range(per):
-            col = (p * per + k) * LANE
-            tmp[pl.ds(k, LANE, stride=per), :] = part[:, col : col + LANE]
-        sums[0, p, 0 : per * LANE] = tmp[...].astype(BF)
-        sums[0, p, per * LANE :] = count.astype(BF)
-    for q in range(1, PLANE):
-        to = lax.rem(place.flip(q), PLANE)
-        net.send(("sums", q), sums.at[0, to], sums.at[1, q], place.peer(q))
+            tmp[q, pl.ds(k, LANE, stride=per), :] = got[:, k * LANE : (k + 1) * LANE]
+        sums[0, to, 0:16] = count
+        sums[0, to, 16:] = tmp[q].astype(BF)
+        if q:
+            send_sums(0, q)
+    for q in (3, 1, 2):
+        send_sums(1, q)
 
     half = SMALL_ROWS // 2
     plane_rows = half // place.lines
@@ -445,6 +463,7 @@
     small[7 * LANE :] = jnp.concatenate(rows, axis=0)
     net.send(("small", "sib"), small.at[aligned(1 - s, half)], small_in, place.sibling)
 
+    q_me = lax.rem(c, PLANE)
     back1 = [to_source_tile(0, e) for e in range(2)]
     net.wait(("small", "sib"), small_in, place.sibling)
     small_lo[...] = (small[aligned(s, half), :] + small_in[...]).astype(BF)
@@ -457,13 +476,82 @@
             small_line.at[line],
             place.peer(line * PLANE),
         )
-    back1.append(to_source_tile(0, 2))
+
+    size = full_out.shape[1]
+    tail = size // 8 // 16 * 16
+    top = size - tail
+    cut = (mid // 32 * 16, mid + (top - mid) // 32 * 16)
+    halves = (
+        (pl.ds(0, cut[0]), pl.ds(cut[0], mid - cut[0])),
+        (pl.ds(mid, cut[1] - mid), pl.ds(cut[1], top - cut[1])),
+    )
+    chunk = (pl.ds(0, mid), pl.ds(mid, top - mid))
+    last = pl.ds(top, tail)
+    order = ((1, 0), (2, 1), (1, 1), (2, 0))
+
+    def out_begin(ch):
+        def along(line):
+            ref = full_out.at[me, chunk[ch]]
+            net.send(("out", ch, line), ref, ref, place.peer(line * PLANE))
+
+        along(1)
+        for q, a in order:
+            ref = full_out.at[me, halves[ch][a]]
+            net.send(("out", ch, 0, q, a), ref, ref, place.peer(q))
+        for line in range(2, place.lines):
+            along(line)
+
+    def out_line(ch, line):
+        mask = line * PLANE
+        blk = place.block(mask)
+        net.wait(("out", ch, line), full_out.at[blk, chunk[ch]], place.peer(mask))
+        for q, a in order:
+            ref = full_out.at[blk, halves[ch][a]]
+            net.send(("out", ch, line, q, a), ref, ref, place.peer(q))
+
+    def out_cross(ch, line):
+        for q, a in ((1, 0), (2, 1)):
+            ref = full_out.at[place.block(line * PLANE + q), halves[ch][a]]
+            net.wait(("out", ch, line, q, a), ref, place.peer(q))
+            net.send(("out", ch, line, 3, a), ref, ref, place.peer(3 - q))
+
+    def last_planes():
+        for q in range(1, PLANE):
+            ref = full_out.at[me, last]
+            net.send(("last", 0, q), ref, ref, place.peer(q))
+
+    def last_lines():
+        for q in range(1, PLANE):
+            net.wait(("last", 0, q), full_out.at[place.block(q), last], place.peer(q))
+        ref = full_out.at[pl.ds(place.level(0), PLANE), last]
+        for line in range(1, place.lines):
+            net.send(("last", line), ref, ref, place.peer(line * PLANE))
+
+    def out_level(line):
+        for ch in range(2):
+            for q, a in ((1, 1), (2, 0)):
+                ref = full_out.at[place.block(line * PLANE + q), halves[ch][a]]
+                net.wait(("out", ch, line, q, a), ref, place.peer(q))
+            for q, a in ((2, 0), (1, 1)):
+                ref = full_out.at[place.block(line * PLANE + 3), halves[ch][a]]
+                net.wait(("out", ch, line, 3, a), ref, place.peer(q))
+        if line > 0:
+            part = full_out.at[pl.ds(place.level(line), PLANE), last]
+            net.wait(("last", line), part, place.peer(line * PLANE))
+        ref = full_out.at[pl.ds(place.level(line), PLANE)]
+        net.send(("out", "sib", line), ref, ref, place.sibling)
+
+    net.settle(early)
+    total = add_sums(0)
+    scale = 1.0 / jnp.sum(total[0:1], axis=1, keepdims=True)
+    full_out[me, 0:mid] = (total[16:] * scale).astype(BF)
+    out_begin(0)
+    back1 += [to_source_tile(0, e) for e in range(2, 4)]
     own = small_lo[aligned(z, plane_rows), :].astype(F32)
     for line in range(1, place.lines):
         net.wait(("small", "line", line), small_line.at[line], place.peer(line * PLANE))
         own = own + small_line[line].astype(F32)
     small_line[0] = own.astype(BF)
-    q_me = lax.rem(c, PLANE)
     for q in range(1, PLANE):
         to = lax.rem(place.flip(q), PLANE)
         net.send(
@@ -472,25 +560,11 @@
             small_plane.at[q],
             place.peer(q),
         )
-    total = sums[0, q_me].astype(F32)
-    for q in range(1, PLANE):
-        net.wait(("sums", q), sums.at[1, q], place.peer(q))
-        total = total + sums[1, q].astype(F32)
-    scale = 1.0 / jnp.sum(total[per * LANE : per * LANE + 1], axis=1, keepdims=True)
-    full_out[me, 0 : per * LANE] = (total[0 : per * LANE] * scale).astype(BF)
-
-    size = full_out.shape[1]
-    mine = full_out.at[me]
-    tail = size // 5 // 16 * 16
-    cut = (size - tail) // 32 * 16
-    halves = (pl.ds(0, cut), pl.ds(cut, size - tail - cut))
-    head, last = pl.ds(0, size - tail), pl.ds(size - tail, tail)
-    net.send(("out", 1), mine.at[head], full_out.at[me, head], place.peer(PLANE))
-    for q, a in ((1, 0), (2, 1), (1, 1), (2, 0)):
-        net.send(("out", 0, q, a), mine.at[halves[a]], full_out.at[me, halves[a]], place.peer(q))
-    for line in range(2, place.lines):
-        net.send(("out", line), mine.at[head], full_out.at[me, head], place.peer(line * PLANE))
-    back1 += [to_source_tile(0, e) for e in range(3, tiles5)]
+    full_out[me, mid : per * LANE] = (add_sums(1) * scale).astype(BF)
+    out_begin(1)
+    mark = len(net.sent)
+    out_cross(0, 0)
+    back1 += [to_source_tile(0, e) for e in range(4, tiles5)]
     d0 = dh1 + to_nodes(back1)
 
     zero = s == 0
@@ -502,63 +576,36 @@
         net.wait(("small", "plane", q), small_plane.at[q], place.peer(q))
         own = own + small_plane[q].astype(F32)
     full_out[me, per * LANE : per * LANE + own_rows] = (own * scale).astype(BF)
-    for q in range(1, PLANE):
-        net.send(("last", 0, q), mine.at[last], full_out.at[me, last], place.peer(q))
-
-    def out_line(line):
-        mask = line * PLANE
-        blk = place.block(mask)
-        net.wait(("out", line), full_out.at[blk, head], place.peer(mask))
-        for q, a in ((1, 0), (2, 1), (1, 1), (2, 0)):
-            ref = full_out.at[blk, halves[a]]
-            net.send(("out", line, q, a), ref, ref, place.peer(q))
-
-    def out_cross(line):
-        for q, a in ((1, 0), (2, 1)):
-            ref = full_out.at[place.block(line * PLANE + q), halves[a]]
-            net.wait(("out", line, q, a), ref, place.peer(q))
-            net.send(("out", line, 3, a), ref, ref, place.peer(3 - q))
-
-    def last_lines():
-        for q in range(1, PLANE):
-            net.wait(("last", 0, q), full_out.at[place.block(q), last], place.peer(q))
-        ref = full_out.at[pl.ds(place.level(0), PLANE), last]
-        for line in range(1, place.lines):
-            net.send(("last", line), ref, ref, place.peer(line * PLANE))
-
-    def out_level(line):
-        for q, a in ((1, 1), (2, 0)):
-            ref = full_out.at[place.block(line * PLANE + q), halves[a]]
-            net.wait(("out", line, q, a), ref, place.peer(q))
-        for q, a in ((2, 0), (1, 1)):
-            ref = full_out.at[place.block(line * PLANE + 3), halves[a]]
-            net.wait(("out", line, 3, a), ref, place.peer(q))
-        ref = full_out.at[pl.ds(place.level(line), PLANE)]
-        if line > 0:
-            part = full_out.at[pl.ds(place.level(line), PLANE), last]
-            net.wait(("last", line), part, place.peer(line * PLANE))
-        net.send(("out", "sib", line), ref, ref, place.sibling)
-
-    loop(3, back_hidden)
-    out_cross(0)
-    loop(2, lambda ib: back_hidden(ib + 3))
-    out_line(1)
+    last_planes()
+    out_line(0, 1)
+    out_cross(1, 0)
+    loop(2, back_hidden)
+    for line in range(2, place.lines):
+        out_line(0, line)
+    out_line(1, 1)
+    out_cross(0, 1)
     last_lines()
-    loop(rounds - 5, lambda ib: back_hidden(ib + 5))
+    loop(3, lambda ib: back_hidden(ib + 2))
+    for line in range(2, place.lines):
+        out_line(1, line)
+    out_cross(1, 1)
+    out_cross(0, 2)
+    out_level(0)
+    net.settle(mark)
+    mark = len(net.sent)
+    loop(LANE // 16 - 5, lambda ib: back_hidden(ib + 5))
     zp = zpre_s[...]
     sig = jax.nn.sigmoid(zp)
     slope = sig * (1.0 + zp * (1.0 - sig))
     lhs = jnp.concatenate(
         [feats, jnp.ones((1, edges), BF), jnp.zeros((15, edges), BF)], axis=0
     )
-    total = jnp.zeros((32, LANE), F32)
-    for t in range(2):
-        dzpre = (dzacc[:, t * edges : (t + 1) * edges] * slope).astype(BF)
-        total = total + dot(lhs, dzpre, 1, 1)
+    total = dot(lhs, (dzacc[...] * slope).astype(BF), 1, 1)
     w1_io[0] = total[0:24]
     net.send(("w1", "sib"), w1_io.at[0], w1_io.at[1], place.sibling)
-    out_cross(1)
-    out_level(0)
+    for line in range(3, place.lines):
+        out_cross(0, line)
+    out_cross(1, 2)
     net.wait(("w1", "sib"), w1_io.at[1], place.sibling)
     total = w1_io[0] + w1_io[1]
     w1_io[2] = total
@@ -572,8 +619,8 @@
     states_out[1] = jnp.where(zero, swap[1, 0], mine_state)
     grads_out[0] = jnp.where(zero, mine_grad, swap[1, 1])
     grads_out[1] = jnp.where(zero, swap[1, 1], mine_grad)
-    for line in range(2, place.lines):
-        out_line(line)
+    for line in range(3, place.lines):
+        out_cross(1, line)
     out_level(1)
     for line in range(1, place.lines):
         net.wait(("w1", "line", line), w1_io.at[at + line], place.peer(line * PLANE))
@@ -582,14 +629,13 @@
     at += place.lines
     for q in range(1, PLANE):
         net.send(("w1", "plane", q), w1_io.at[3], w1_io.at[at + q], place.peer(q))
+    net.settle(mark)
     for line in range(2, place.lines):
-        out_cross(line)
+        out_level(line)
     for q in range(1, PLANE):
         net.wait(("w1", "plane", q), w1_io.at[at + q], place.peer(q))
         total = total + w1_io[at + q]
     w1_out[...] = total * scale
-    for line in range(2, place.lines):
-        out_level(line)
     for line in range(place.lines):
         first = place.level(line) + (1 - 2 * s) * parts
         net.wait(("out", "sib", line), full_out.at[pl.ds(first, PLANE)], place.sibling)
@@ -667,12 +713,13 @@
             VMEM((width, edges), F32), VMEM((2, width, edges), F32),
             VMEM((width, 2 * edges), BF), VMEM((2, width, edges), F32),
             VMEM((width, 2 * edges), BF),
-            VMEM((width, 2 * edges), F32), VMEM((nodes, edges), BF), VMEM((nodes, edges), BF),
+            VMEM((width, edges), F32), VMEM((nodes, edges), BF), VMEM((nodes, edges), BF),
             VMEM((group, 16 * (edges // LANE + 1), LANE), BF),
             VMEM((2, group, nodes, width), BF), VMEM((2, group, width, nodes), BF),
             VMEM((2, group * nodes, units * width), BF), VMEM((group, units, edges), F32),
             VMEM((width, units * width), F32),
-            VMEM((2, PLANE, per * width + 16, width), BF), VMEM((width * per, width), F32),
+            VMEM((2, PLANE, per * width + 16, width), BF),
+            VMEM((PLANE, width * per, width), F32),
             VMEM((SMALL_ROWS, width), F32), VMEM((half, width), F32),
             VMEM((half, width), BF), VMEM((lines, plane_rows, width), BF),
             VMEM((PLANE, own_rows, width), BF), VMEM((4 + lines + PLANE, 24, width), F32),

time: 79 us -> 74.7 us (0.946)
  Pallas kernels: 78.2 us -> 73.9 us
    pallas_call x1, Pallas kernels: 73.8 us -> 69.6 us  [shards(): pl.pallas_call(main_kernel, out_shape=(VMEM((blocks, size, width), BF), V...]
where the time goes in v4:
time: 74.7 us; the launch traced here: 74.6 us
  Pallas kernels  73.9 us (99%)
    pallas_call x1, Pallas kernels, shards(): pl.pallas_call(main_kernel, out_shape=(VMEM((blocks, size, width), BF), V...  69.6 us
    pallas_call x1, Pallas kernels, shards(): pl.pallas_call(final_kernel, out_shape=(sds((width, width * width), F32),...  4.35 us

profile of v4, /device:TPU:0, one launch (start us, length us, event | category | flops | bytes accessed | tf_op | source)
XLA Modules:
  0.0 74.6 jit_solution(1586993065667962930)
XLA Ops:
  0.6 69.6 %shard_map.222 = (bf16[32,544,128]{2,1,0:T(8,128)(2,1)S(1)}, f32[2,128,128]{2,1,0:T(8,128)S(1)}, f32[2,128,128]{2,1,0:T(8,128)S(1)}, f32[24,128]{1,0:T(8,128)S(1)}) custom-call(bf16[2,128,128]{2,1,0:T(8,128)(2,1)} %x_ref.1, bf16[2,16,640]{2,1,0:T(8,128)(2,1)} %f_ref.1, s32[2,640]{1,0:T(2,128)} %src_ref.1, s32[2,640]{1,0:T(2,128)} %tgt_ref.1, ...), custom_call_target="tpu_custom_call" | custom-call | tf_op jit(solution)/shard_map/pallas_call | solution.py:702
  70.2 4.4 %shard_map.223 = (f32[128,16384]{1,0:T(8,128)}, f32[128,128]{1,0:T(8,128)}, f32[128,384]{1,0:T(8,128)}, f32[384]{0:T(512)}, f32[128,384]{1,0:T(8,128)}, /*index=...) custom-call(bf16[32,544,128]{2,1,0:T(8,128)(2,1)S(1)} %get-tuple-element.24.f, ...), custom_call_target="tpu_custom_call" | custom-call | tf_op jit(solution)/shard_map/pallas_call | solution.py:739

commit v5 on v4

--- a/solution.py
+++ b/solution.py
@@ -407,7 +407,12 @@
 
     for blk in range(group):
         hidden(blk)
-    loop(group, build)
+
+    def build_pair(b):
+        build(2 * b)
+        build(2 * b + 1)
+
+    loop(group // 2, build_pair)
     gather_d1.middle()
     gather_d2.finish()
     lhs = jnp.concatenate([dts[1, blk] for blk in range(group)], axis=1)
@@ -487,7 +492,6 @@
     )
     chunk = (pl.ds(0, mid), pl.ds(mid, top - mid))
     last = pl.ds(top, tail)
-    order = ((1, 0), (2, 1), (1, 1), (2, 0))
 
     def out_begin(ch):
         def along(line):
@@ -495,9 +499,9 @@
             net.send(("out", ch, line), ref, ref, place.peer(line * PLANE))
 
         along(1)
-        for q, a in order:
-            ref = full_out.at[me, halves[ch][a]]
-            net.send(("out", ch, 0, q, a), ref, ref, place.peer(q))
+        for q in (1, 2):
+            ref = full_out.at[me, chunk[ch]]
+            net.send(("out", ch, 0, q), ref, ref, place.peer(q))
         for line in range(2, place.lines):
             along(line)
 
@@ -505,14 +509,15 @@
         mask = line * PLANE
         blk = place.block(mask)
         net.wait(("out", ch, line), full_out.at[blk, chunk[ch]], place.peer(mask))
-        for q, a in order:
-            ref = full_out.at[blk, halves[ch][a]]
-            net.send(("out", ch, line, q, a), ref, ref, place.peer(q))
+        for q in (1, 2):
+            ref = full_out.at[blk, chunk[ch]]
+            net.send(("out", ch, line, q), ref, ref, place.peer(q))
 
     def out_cross(ch, line):
         for q, a in ((1, 0), (2, 1)):
-            ref = full_out.at[place.block(line * PLANE + q), halves[ch][a]]
-            net.wait(("out", ch, line, q, a), ref, place.peer(q))
+            blk = place.block(line * PLANE + q)
+            net.wait(("out", ch, line, q), full_out.at[blk, chunk[ch]], place.peer(q))
+            ref = full_out.at[blk, halves[ch][a]]
             net.send(("out", ch, line, 3, a), ref, ref, place.peer(3 - q))
 
     def last_planes():
@@ -529,9 +534,6 @@
 
     def out_level(line):
         for ch in range(2):
-            for q, a in ((1, 1), (2, 0)):
-                ref = full_out.at[place.block(line * PLANE + q), halves[ch][a]]
-                net.wait(("out", ch, line, q, a), ref, place.peer(q))
             for q, a in ((2, 0), (1, 1)):
                 ref = full_out.at[place.block(line * PLANE + 3), halves[ch][a]]
                 net.wait(("out", ch, line, 3, a), ref, place.peer(q))
@@ -579,21 +581,20 @@
     last_planes()
     out_line(0, 1)
     out_cross(1, 0)
-    loop(2, back_hidden)
+    loop(3, back_hidden)
     for line in range(2, place.lines):
         out_line(0, line)
     out_line(1, 1)
     out_cross(0, 1)
     last_lines()
-    loop(3, lambda ib: back_hidden(ib + 2))
+    loop(3, lambda ib: back_hidden(ib + 3))
     for line in range(2, place.lines):
         out_line(1, line)
     out_cross(1, 1)
     out_cross(0, 2)
     out_level(0)
-    net.settle(mark)
     mark = len(net.sent)
-    loop(LANE // 16 - 5, lambda ib: back_hidden(ib + 5))
+    loop(LANE // 16 - 6, lambda ib: back_hidden(ib + 6))
     zp = zpre_s[...]
     sig = jax.nn.sigmoid(zp)
     slope = sig * (1.0 + zp * (1.0 - sig))

time: 74.7 us -> 73.3 us (0.981)
  Pallas kernels: 73.9 us -> 72.3 us
    pallas_call x1, Pallas kernels: 69.6 us -> 68 us  [shards(): pl.pallas_call(main_kernel, out_shape=(VMEM((blocks, size, width), BF), V...]
where the time goes in v5:
time: 73.3 us; the launch traced here: 73.1 us
  Pallas kernels  72.3 us (99%)
  between operations  0.82 us (1%)
    pallas_call x1, Pallas kernels, shards(): pl.pallas_call(main_kernel, out_shape=(VMEM((blocks, size, width), BF), V...  68 us
    pallas_call x1, Pallas kernels, shards(): pl.pallas_call(final_kernel, out_shape=(sds((width, width * width), F32),...  4.35 us

profile of v5, /device:TPU:0, one launch (start us, length us, event | category | flops | bytes accessed | tf_op | source)
XLA Modules:
  0.0 73.1 jit_solution(2811321699666269013)
XLA Ops:
  0.6 68.0 %shard_map.222 = (bf16[32,544,128]{2,1,0:T(8,128)(2,1)S(1)}, f32[2,128,128]{2,1,0:T(8,128)S(1)}, f32[2,128,128]{2,1,0:T(8,128)S(1)}, f32[24,128]{1,0:T(8,128)S(1)}) custom-call(bf16[2,128,128]{2,1,0:T(8,128)(2,1)} %x_ref.1, bf16[2,16,640]{2,1,0:T(8,128)(2,1)} %f_ref.1, s32[2,640]{1,0:T(2,128)} %src_ref.1, s32[2,640]{1,0:T(2,128)} %tgt_ref.1, ...), custom_call_target="tpu_custom_call" | custom-call | tf_op jit(solution)/shard_map/pallas_call | solution.py:703
  68.6 4.4 %shard_map.223 = (f32[128,16384]{1,0:T(8,128)}, f32[128,128]{1,0:T(8,128)}, f32[128,384]{1,0:T(8,128)}, f32[384]{0:T(512)}, f32[128,384]{1,0:T(8,128)}, /*index=...) custom-call(bf16[32,544,128]{2,1,0:T(8,128)(2,1)S(1)} %get-tuple-element.24.f, ...), custom_call_target="tpu_custom_call" | custom-call | tf_op jit(solution)/shard_map/pallas_call | solution.py:740

commit v6 on v5

--- a/solution.py
+++ b/solution.py
@@ -581,20 +581,20 @@
     last_planes()
     out_line(0, 1)
     out_cross(1, 0)
-    loop(3, back_hidden)
+    loop(4, back_hidden)
     for line in range(2, place.lines):
         out_line(0, line)
     out_line(1, 1)
     out_cross(0, 1)
     last_lines()
-    loop(3, lambda ib: back_hidden(ib + 3))
+    loop(3, lambda ib: back_hidden(ib + 4))
     for line in range(2, place.lines):
         out_line(1, line)
     out_cross(1, 1)
     out_cross(0, 2)
     out_level(0)
     mark = len(net.sent)
-    loop(LANE // 16 - 6, lambda ib: back_hidden(ib + 6))
+    loop(LANE // 16 - 7, lambda ib: back_hidden(ib + 7))
     zp = zpre_s[...]
     sig = jax.nn.sigmoid(zp)
     slope = sig * (1.0 + zp * (1.0 - sig))

time: 73.3 us -> 73.8 us (level)
  no operation moved by 1% of the time
where the time goes in v6:
time: 73.8 us; the launch traced here: 73.6 us
  Pallas kernels  72.8 us (99%)
  between operations  0.82 us (1%)
    pallas_call x1, Pallas kernels, shards(): pl.pallas_call(main_kernel, out_shape=(VMEM((blocks, size, width), BF), V...  68.5 us
    pallas_call x1, Pallas kernels, shards(): pl.pallas_call(final_kernel, out_shape=(sds((width, width * width), F32),...  4.35 us

profile of v6, /device:TPU:0, one launch (start us, length us, event | category | flops | bytes accessed | tf_op | source)
XLA Modules:
  0.0 73.6 jit_solution(12089710609802311788)
XLA Ops:
  0.6 68.5 %shard_map.222 = (bf16[32,544,128]{2,1,0:T(8,128)(2,1)S(1)}, f32[2,128,128]{2,1,0:T(8,128)S(1)}, f32[2,128,128]{2,1,0:T(8,128)S(1)}, f32[24,128]{1,0:T(8,128)S(1)}) custom-call(bf16[2,128,128]{2,1,0:T(8,128)(2,1)} %x_ref.1, bf16[2,16,640]{2,1,0:T(8,128)(2,1)} %f_ref.1, s32[2,640]{1,0:T(2,128)} %src_ref.1, s32[2,640]{1,0:T(2,128)} %tgt_ref.1, ...), custom_call_target="tpu_custom_call" | custom-call | tf_op jit(solution)/shard_map/pallas_call | solution.py:703
  69.1 4.4 %shard_map.223 = (f32[128,16384]{1,0:T(8,128)}, f32[128,128]{1,0:T(8,128)}, f32[128,384]{1,0:T(8,128)}, f32[384]{0:T(512)}, f32[128,384]{1,0:T(8,128)}, /*index=...) custom-call(bf16[32,544,128]{2,1,0:T(8,128)(2,1)S(1)} %get-tuple-element.24.f, ...), custom_call_target="tpu_custom_call" | custom-call | tf_op jit(solution)/shard_map/pallas_call | solution.py:740
